TPU v7x, 32 devices: a whole 2x2x4 slice. The times are simulated.
32 devices in a mesh: section: 2 (over core), dp: 16 (over z, y, x).
Axes of the slice: x: 2, y: 2, z: 4, core: 2. Of those that a mesh axis runs over, the one named last changes fastest.
Arguments:
- frames: float32 [2, 16, 256, 1024], P(None, 'dp')
- cotangent: float32 [2, 16, 256, 1024], P(None, 'dp'), may hold values from -6 to 6
- lengths: int32 [2, 16], P(None, 'dp'), may hold values from 1 to 256, 2560 in all within a row
- attn_in: float32 [2, 1024, 3072], P('section', 'dp')
- attn_out: float32 [2, 1024, 1024], P('section', 'dp')
- ffn_up: float32 [2, 1024, 4096], P('section', 'dp')
- ffn_down: float32 [2, 4096, 1024], P('section', 'dp')
- norm_params: float32 [2, 4, 1024], P('section', None, 'dp')
- skip_proj: float32 [2048, 1024], P(('section', 'dp'))
- in_rows: float32 [2, 1024], P('section', 'dp'), may hold values from 491.52 to 1966.08
- in_cols: float32 [2, 3072], P('section'), may hold values from 491.52 to 1966.08
- out_rows: float32 [2, 1024], P('section', 'dp'), may hold values from 98.304 to 393.216
- out_cols: float32 [2, 1024], P('section'), may hold values from 98.304 to 393.216
- up_rows: float32 [2, 1024], P('section', 'dp'), may hold values from 98.304 to 393.216
- up_cols: float32 [2, 4096], P('section'), may hold values from 98.304 to 393.216
- down_rows: float32 [2, 4096], P('section', 'dp'), may hold values from 393.216 to 1572.864
- down_cols: float32 [2, 1024], P('section'), may hold values from 393.216 to 1572.864
- skip_rows: float32 [2048], P(('section', 'dp')), may hold values from 1966.08 to 7864.32
- skip_cols: float32 [1024], replicated, may hold values from 1966.08 to 7864.32
- norm_moment: float32 [2, 4, 1024], P('section', None, 'dp'), may hold values from 983.04 to 3932.16
Outputs:
- layer_outputs: float32 [2, 2, 16, 256, 1024], P('section', None, 'dp')
- input_grads: float32 [2, 2, 16, 256, 1024], P('section', None, 'dp')
- grad_in: float32 [2, 1024, 3072], P('section', 'dp')
- rows_in: float32 [2, 1024], P('section', 'dp')
- cols_in: float32 [2, 3072], P('section')
- new_in: float32 [2, 1024, 3072], P('section', 'dp')
- grad_out: float32 [2, 1024, 1024], P('section', 'dp')
- rows_out: float32 [2, 1024], P('section', 'dp')
- cols_out: float32 [2, 1024], P('section')
- new_out: float32 [2, 1024, 1024], P('section', 'dp')
- grad_up: float32 [2, 1024, 4096], P('section', 'dp')
- rows_up: float32 [2, 1024], P('section', 'dp')
- cols_up: float32 [2, 4096], P('section')
- new_up: float32 [2, 1024, 4096], P('section', 'dp')
- grad_down: float32 [2, 4096, 1024], P('section', 'dp')
- rows_down: float32 [2, 4096], P('section', 'dp')
- cols_down: float32 [2, 1024], P('section')
- new_down: float32 [2, 4096, 1024], P('section', 'dp')
- grad_skip: float32 [2048, 1024], P(('section', 'dp'))
- rows_skip: float32 [2048], P(('section', 'dp'))
- cols_skip: float32 [1024], replicated
- new_skip: float32 [2048, 1024], P(('section', 'dp'))
- grad_norms: float32 [2, 4, 1024], P('section', None, 'dp')
- moment_norms: float32 [2, 4, 1024], P('section', None, 'dp')
- new_norms: float32 [2, 4, 1024], P('section', None, 'dp')
Inputs may be any that keep to these rules, and one draw needn't show every extreme that they name: In every micro-batch the lengths sum to 2560 and one equals 256.
All inputs are finite; a program needn't handle non-finite values. No bound on the sum of `lengths` on one device may be relied on, other than what follows from the above.
Results may differ from a plain program's by a relative error of at most 0.0003.
Values sent between devices are 32-bit elements; how exact they have to be, the bound alone decides.
No kernel may reach another device: no remote copies, remote signals or barrier semaphores. Data moves between devices by JAX's collectives and lax.ppermute only.
A program may use at most 896 MiB of HBM per device.

v0:
```python
from functools import partial

import jax
import jax.numpy as jnp
from jax import lax
from jax.sharding import PartitionSpec as P

HEADS = 16
STEP = 10


EPS = 1e-05
TINY = 1e-30
CLIP = 1.0
RHO = 0.5
FLOOR = 0.001
MASKED = -1e30
HIGH = lax.Precision.HIGHEST


def from_partner(block, axis, distance):
    count = lax.axis_size(axis)
    route = []
    for low in range(count):
        high = low | 1 << distance
        if high != low and high < count:
            route += [(low, high), (high, low)]
    return lax.ppermute(block, axis, route)


def layer_norm(stream, norm_gain, norm_shift):
    average = jnp.mean(stream, axis=-1, keepdims=True)
    centered = stream - average
    spread = jnp.mean(centered * centered, axis=-1, keepdims=True)
    return centered * lax.rsqrt(spread + EPS) * norm_gain + norm_shift


def attention(stream, norm_gain, norm_shift, w_in, w_out, length):
    frame_count, model_width = stream.shape
    head_width = model_width // HEADS
    normed = layer_norm(stream, norm_gain, norm_shift)
    projected = jnp.dot(normed, w_in, precision=HIGH).reshape(frame_count, 3, HEADS, head_width)
    query_heads = projected[:, 0]
    key_heads = projected[:, 1]
    value_heads = projected[:, 2]
    scores = jnp.einsum("qhd,khd->hqk", query_heads, key_heads, precision=HIGH) * head_width ** (
        -0.5
    )
    positions = jnp.arange(frame_count)
    distance = jnp.abs(positions[:, None] - positions[None, :]).astype(jnp.float32)
    slopes = 2.0 ** (-8.0 * (jnp.arange(HEADS).astype(jnp.float32) + 1.0) / HEADS)
    scores = scores - slopes[:, None, None] * distance[None]
    scores = jnp.where((positions < length)[None, None, :], scores, MASKED)
    row_max = jnp.max(scores, axis=-1, keepdims=True)
    weighted = jnp.exp(scores - row_max)
    probability = weighted / jnp.sum(weighted, axis=-1, keepdims=True)
    context = jnp.einsum("hqk,khd->qhd", probability, value_heads, precision=HIGH).reshape(
        frame_count, model_width
    )
    return stream + jnp.dot(context, w_out, precision=HIGH)


def feed_forward(stream, norm_gain, norm_shift, w_up, w_down):
    normed = layer_norm(stream, norm_gain, norm_shift)
    hidden = jax.nn.gelu(jnp.dot(normed, w_up, precision=HIGH), approximate=False)
    return stream + jnp.dot(hidden, w_down, precision=HIGH)


def section_zero(params, received, source, earlier, length, with_ffn, with_attn):
    w_in, w_out, w_up, w_down, norm_set, w_skip = params
    if with_ffn:
        result = feed_forward(received, norm_set[2], norm_set[3], w_up, w_down)
    else:
        result = jnp.zeros_like(received)
    if with_attn:
        sending = attention(source, norm_set[0], norm_set[1], w_in, w_out, length)
    else:
        sending = jnp.zeros_like(source)
    return (sending, result)


def section_one(params, received, source, earlier, length, active):
    w_in, w_out, w_up, w_down, norm_set, w_skip = params
    if active:
        mixed_out = feed_forward(received, norm_set[2], norm_set[3], w_up, w_down)
        joined = jnp.dot(jnp.concatenate([mixed_out, earlier], axis=-1), w_skip, precision=HIGH)
        sending = attention(joined, norm_set[0], norm_set[1], w_in, w_out, length)
        return (sending, mixed_out)
    return (jnp.zeros_like(received), jnp.zeros_like(received))


def local_moments(grad, rows_old):
    decay = 1.0 - STEP ** (-0.8)
    squared = grad * grad + TINY
    rows_new = decay * rows_old + (1.0 - decay) * jnp.mean(squared, axis=1)
    return (rows_new, jnp.sum(squared, axis=0), jnp.sum(grad * grad / rows_new[:, None], axis=0))


def raw_update(grad, rows_new, cols_old, column_total, rows_total, total_rows):
    decay = 1.0 - STEP ** (-0.8)
    cols_new = decay * cols_old + (1.0 - decay) * (column_total / total_rows)
    second = rows_new[:, None] * cols_new[None, :] / (rows_total / total_rows)
    return (cols_new, grad * lax.rsqrt(second))


def apply_update(weight, update, update_total, weight_total, element_count):
    ratio = jnp.sqrt(update_total / element_count) / CLIP
    scale = jnp.maximum(jnp.sqrt(weight_total / element_count), FLOOR)
    return weight - RHO * scale * (update / jnp.maximum(ratio, 1.0))


def norm_local(grad, moment):
    decay = 1.0 - STEP ** (-0.8)
    moment_new = decay * moment + (1.0 - decay) * (grad * grad + TINY)
    return (moment_new, grad * lax.rsqrt(moment_new))


def on_device(
    frames,
    cotangent,
    lengths,
    attn_in,
    attn_out,
    ffn_up,
    ffn_down,
    norm_params,
    skip_proj,
    in_rows,
    in_cols,
    out_rows,
    out_cols,
    up_rows,
    up_cols,
    down_rows,
    down_cols,
    skip_rows,
    skip_cols,
    norm_moment,
):
    micro_count = frames.shape[0]
    frame_count = frames.shape[2]
    model_width = frames.shape[3]
    second_section = lax.axis_index("section") == 1
    stacked = (
        lax.all_gather(attn_in, "dp", axis=1, tiled=True),
        lax.all_gather(attn_out, "dp", axis=1, tiled=True),
        lax.all_gather(ffn_up, "dp", axis=1, tiled=True),
        lax.all_gather(ffn_down, "dp", axis=1, tiled=True),
        lax.all_gather(norm_params, "dp", axis=2, tiled=True),
    )
    skip_full = lax.all_gather(skip_proj, ("section", "dp"), axis=0, tiled=True)
    params = (stacked[0][0], stacked[1][0], stacked[2][0], stacked[3][0], stacked[4][0], skip_full)

    def run_instant(params_now, received, source, earlier, instant):
        first_length = lengths[min(instant, micro_count - 1), 0]
        second_length = lengths[min(max(instant - 1, 0), micro_count - 1), 0]
        branch_one = partial(section_one, length=second_length, active=1 <= instant <= micro_count)
        branch_zero = partial(
            section_zero,
            length=first_length,
            with_ffn=instant >= 2,
            with_attn=instant < micro_count,
        )
        return lax.cond(
            second_section, branch_one, branch_zero, params_now, received, source, earlier
        )

    received = jnp.zeros((frame_count, model_width), jnp.float32)
    pullbacks = []
    inputs = []
    results = []
    for instant in range(micro_count + 2):
        source = frames[min(instant, micro_count - 1), 0]
        earlier = frames[min(max(instant - 1, 0), micro_count - 1), 0]
        handler = partial(run_instant, instant=instant)
        (sending, result), pullback = jax.vjp(handler, params, received, source, earlier)
        pullbacks.append(pullback)
        inputs.append(received)
        results.append(result)
        if instant <= micro_count:
            received = from_partner(sending, "section", 0)
    layer_list = [
        jnp.where(second_section, results[member + 1], results[member + 2])
        for member in range(micro_count)
    ]
    layer_outputs = jnp.stack(layer_list)[None, :, None]
    gradients = jax.tree.map(jnp.zeros_like, params)
    sent_grad = jnp.zeros((frame_count, model_width), jnp.float32)
    sent_early = jnp.zeros((frame_count, model_width), jnp.float32)
    source_grads = [None] * (micro_count + 2)
    received_grads = [None] * (micro_count + 2)
    for instant in reversed(range(micro_count + 2)):
        if instant >= 2:
            valid_rows = (jnp.arange(frame_count) < lengths[instant - 2, 0]).astype(jnp.float32)[
                :, None
            ]
            result_grad = jnp.where(second_section, 0.0, cotangent[instant - 2, 0] * valid_rows)
        else:
            result_grad = jnp.zeros((frame_count, model_width), jnp.float32)
        pullback = pullbacks[instant]
        param_grad, received_grad, source_grad, early_grad = pullback((sent_grad, result_grad))
        gradients = jax.tree.map(jnp.add, gradients, param_grad)
        source_grads[instant] = source_grad + sent_early
        received_grads[instant] = received_grad
        if instant >= 1:
            sent_grad, sent_early = from_partner((received_grad, early_grad), "section", 0)
    grad_list = [
        jnp.where(second_section, received_grads[member + 1], source_grads[member])
        for member in range(micro_count)
    ]
    input_grads = jnp.stack(grad_list)[None, :, None]
    summed = (
        lax.psum_scatter(gradients[0][None], "dp", scatter_dimension=1, tiled=True),
        lax.psum_scatter(gradients[1][None], "dp", scatter_dimension=1, tiled=True),
        lax.psum_scatter(gradients[2][None], "dp", scatter_dimension=1, tiled=True),
        lax.psum_scatter(gradients[3][None], "dp", scatter_dimension=1, tiled=True),
        lax.psum_scatter(gradients[4][None], "dp", scatter_dimension=2, tiled=True),
    )
    skip_grad = lax.psum_scatter(gradients[5], ("section", "dp"), scatter_dimension=0, tiled=True)
    data_size = lax.axis_size("dp")
    shares = [summed[0][0], summed[1][0], summed[2][0], summed[3][0]]
    norm_share = summed[4][0]
    current = [attn_in[0], attn_out[0], ffn_up[0], ffn_down[0]]
    rows_old = [in_rows[0], out_rows[0], up_rows[0], down_rows[0]]
    cols_old = [in_cols[0], out_cols[0], up_cols[0], down_cols[0]]
    moments = [local_moments(shares[member], rows_old[member]) for member in range(4)]
    row_sums = [jnp.sum(moments[member][0]) for member in range(4)]
    weight_sums = [jnp.sum(current[member] * current[member]) for member in range(4)]
    norm_moment_new, norm_raw = norm_local(norm_share, norm_moment[0])
    norm_update_sq = jnp.sum(norm_raw * norm_raw, axis=-1)
    norm_param_sq = jnp.sum(norm_params[0] * norm_params[0], axis=-1)
    totals = lax.psum(
        (
            moments[0][1],
            row_sums[0],
            weight_sums[0],
            moments[1][1],
            row_sums[1],
            weight_sums[1],
            moments[2][1],
            row_sums[2],
            weight_sums[2],
            moments[3][1],
            row_sums[3],
            weight_sums[3],
            norm_update_sq,
            norm_param_sq,
        ),
        "dp",
    )
    updated = []
    for member in range(4):
        total_rows = shares[member].shape[0] * data_size
        updated.append(
            raw_update(
                shares[member],
                moments[member][0],
                cols_old[member],
                totals[3 * member],
                totals[3 * member + 1],
                total_rows,
            )
        )
    squares_local = [jnp.sum(updated[member][1] * updated[member][1]) for member in range(4)]
    update_totals = lax.psum(
        (squares_local[0], squares_local[1], squares_local[2], squares_local[3]), "dp"
    )
    new_weights = [
        apply_update(
            current[member],
            updated[member][1],
            update_totals[member],
            totals[3 * member + 2],
            shares[member].shape[0] * data_size * shares[member].shape[1],
        )
        for member in range(4)
    ]
    norm_width = norm_share.shape[1] * data_size
    norm_ratio = jnp.sqrt(totals[12] / norm_width) / CLIP
    norm_scale = jnp.maximum(jnp.sqrt(totals[13] / norm_width), FLOOR)
    norms_new = norm_params[0] - RHO * norm_scale[:, None] * (
        norm_raw / jnp.maximum(norm_ratio, 1.0)[:, None]
    )
    every_size = lax.axis_size(("section", "dp"))
    skip_total_rows = skip_grad.shape[0] * every_size
    skip_rows_new, skip_column, skip_scaled = local_moments(skip_grad, skip_rows)
    skip_weight_sq = jnp.sum(skip_proj * skip_proj)
    skip_totals = lax.psum((skip_column, jnp.sum(skip_rows_new), skip_weight_sq), ("section", "dp"))
    skip_cols_new, skip_update = raw_update(
        skip_grad, skip_rows_new, skip_cols, skip_totals[0], skip_totals[1], skip_total_rows
    )
    skip_update_total = lax.psum(jnp.sum(skip_update * skip_update), ("section", "dp"))
    skip_new = apply_update(
        skip_proj,
        skip_update,
        skip_update_total,
        skip_totals[2],
        skip_total_rows * skip_grad.shape[1],
    )
    return (
        layer_outputs,
        input_grads,
        summed[0],
        moments[0][0][None],
        updated[0][0][None],
        new_weights[0][None],
        summed[1],
        moments[1][0][None],
        updated[1][0][None],
        new_weights[1][None],
        summed[2],
        moments[2][0][None],
        updated[2][0][None],
        new_weights[2][None],
        summed[3],
        moments[3][0][None],
        updated[3][0][None],
        new_weights[3][None],
        skip_grad,
        skip_rows_new,
        skip_cols_new,
        skip_new,
        summed[4],
        norm_moment_new[None],
        norms_new[None],
    )


def solution(mesh):
    return jax.shard_map(
        on_device,
        mesh=mesh,
        in_specs=(
            P(None, "dp", None, None),
            P(None, "dp", None, None),
            P(None, "dp"),
            P("section", "dp", None),
            P("section", "dp", None),
            P("section", "dp", None),
            P("section", "dp", None),
            P("section", None, "dp"),
            P(("section", "dp"), None),
            P("section", "dp"),
            P("section", None),
            P("section", "dp"),
            P("section", None),
            P("section", "dp"),
            P("section", None),
            P("section", "dp"),
            P("section", None),
            P(("section", "dp")),
            P(),
            P("section", None, "dp"),
        ),
        out_specs=(
            P("section", None, "dp", None, None),
            P("section", None, "dp", None, None),
            P("section", "dp", None),
            P("section", "dp"),
            P("section", None),
            P("section", "dp", None),
            P("section", "dp", None),
            P("section", "dp"),
            P("section", None),
            P("section", "dp", None),
            P("section", "dp", None),
            P("section", "dp"),
            P("section", None),
            P("section", "dp", None),
            P("section", "dp", None),
            P("section", "dp"),
            P("section", None),
            P("section", "dp", None),
            P(("section", "dp"), None),
            P(("section", "dp")),
            P(),
            P(("section", "dp"), None),
            P("section", None, "dp"),
            P("section", None, "dp"),
            P("section", None, "dp"),
        ),
        check_vma=False,
    )
```

profile of v0, /device:TPU:1, one launch (start us, length us, event | category | flops | bytes accessed | tf_op | source)
XLA Modules:
  0.0 3218.3 jit_solution(18243654372618438186)
XLA Ops:
  11.4 41.3 %all_gather.18 = f32[1,4,1024]{1,0,2:T(1,128)} all-gather(f32[1,4,64]{1,0,2:T(1,128)S(1)} %copy.180), channel_id=1, replica_groups=mesh['section'=2,'dp'=16] {'dp'}, dimensions={2}, use_global_device_ids=true | all-gather | bytes 17408 | tf_op jit(solution)/shard_map/all_gather | solution.py:149
  56.7 34.2 %all-gather.8.cloned.1.call-done = f32[1,1024,1024]{2,1,0:T(8,128)} async-done(((f32[1,64,1024]{2,1,0:T(8,128)}), f32[1,1024,1024]{2,1,0:T(8,128)}) %all-gather.8.cloned.1.call-update) | async-done | bytes 4194320 | tf_op jit(solution)/shard_map/all_gather | solution.py:146
  90.9 154.2 %all-gather.6.cloned.1.call-done = f32[1,1024,3072]{2,1,0:T(8,128)} async-done(((f32[1,64,3072]{2,1,0:T(8,128)}), f32[1,1024,3072]{2,1,0:T(8,128)}) %all-gather.6.cloned.1.call-update) | async-done | bytes 12582928 | tf_op jit(solution)/shard_map/all_gather | solution.py:145
  245.1 33.6 %conditional.10 = (f32[256,1024]{1,0:T(8,128)}, f32[256,1024]{1,0:T(8,128)S(1)}, f32[256,1]{0,1:T(1,128)S(1)}, f32[256,1]{0,1:T(1,128)S(1)}, f32[1,1024]{1,0:T(1...) conditional(s32[]{:T(128)} %convert_element_type.97, ...), branch_computations={%region_0.6_spmd, %region_6.7_spmd} | conditional | flops 14513532928 | bytes 123655304 | solution.py:164
  278.7 43.3 %collective-permute-start = (f32[256,1024]{1,0:T(8,128)}, f32[256,1024]{1,0:T(8,128)}, u32[]{:S(2)}, u32[]{:S(2)}) collective-permute-start(f32[256,1024]{1,0:T(8,128)} %get-tuple-element.756), channel_id=1, source_target_pairs={{0,16},{16,0},{1,17},{17,1},{2,18},{18,2},{3,19},{19,3},{4,20},{20... | collective-permute-start | bytes 3145736 | tf_op jit(solution)/shard_map/ppermute | solution.py:28
  325.6 192.0 %all-gather.10.cloned.1.call-done = f32[1,1024,4096]{2,1,0:T(8,128)} async-done(((f32[1,64,4096]{2,1,0:T(8,128)}), f32[1,1024,4096]{2,1,0:T(8,128)}) %all-gather.10.cloned.1.call-update) | async-done | bytes 16777232 | tf_op jit(solution)/shard_map/all_gather | solution.py:147
  517.6 192.5 %all-gather.12.cloned.1.call-done = f32[1,4096,1024]{2,1,0:T(8,128)} async-done(((f32[1,256,1024]{2,1,0:T(8,128)}), f32[1,4096,1024]{2,1,0:T(8,128)}) %all-gather.12.cloned.1.call-update) | async-done | bytes 16777232 | tf_op jit(solution)/shard_map/all_gather | solution.py:148
  710.1 161.7 %conditional.18 = (f32[256,1024]{1,0:T(8,128)}, f32[256,1024]{1,0:T(8,128)S(1)}, f32[256,1024]{1,0:T(8,128)S(1)}, f32[256,1]{0,1:T(1,128)S(1)}, f32[256,1]{0,1:T...) conditional(s32[]{:T(128)} %convert_element_type.97, ...), branch_computations={%region_7.13_spmd, %region_13.21_spmd} | conditional | flops 46795517952 | bytes 466675776
  875.8 149.7 %conditional.12 = (f32[256,1024]{1,0:T(8,128)S(1)}, f32[256,1024]{1,0:T(8,128)S(1)}, f32[256,1024]{1,0:T(8,128)S(1)}, f32[256,1]{0,1:T(1,128)S(1)}, f32[256,1]{0...) conditional(s32[]{:T(128)} %convert_element_type.97, ...), branch_computations={%region_21.24_spmd, %region_24.32_spmd} | conditional | flops 46795517952 | bytes 349333440 | solution.py:164
  890.1 29.9 fusion.116
  1028.3 31.3 conditional.13
  1080.7 135.1 %collective-permute-start.3 = (f32[256,1024]{1,0:T(8,128)}, f32[256,1024]{1,0:T(8,128)}, u32[]{:S(2)}, u32[]{:S(2)}) collective-permute-start(f32[256,1024]{1,0:T(8,128)} %get-tuple-element.786), channel_id=1, source_target_pairs={{0,16},{16,0},{1,17},{17,1},{2,18},{18,2},{3,19},{19,3},{4,20},{20... | collective-permute-start | bytes 3145736 | tf_op jit(solution)/shard_map/ppermute | solution.py:28
  1218.5 246.1 %conditional.15 = (f32[1024,1024]{1,0:T(8,128)}, f32[256,1024]{1,0:T(8,128)}, f32[4,1024]{1,0:T(4,128)}, f32[]{:T(128)}, f32[256,1024]{1,0:T(8,128)S(1)}, /*inde...) conditional(s32[]{:T(128)} %convert_element_type.97, ...), branch_computations={%region_42.47_spmd.clone, %region_47.58_spmd.clone} | conditional | flops 93448052736 | bytes 405153152 | solution.py:164
  1470.4 244.3 %conditional.16 = (f32[1024,1024]{1,0:T(8,128)}, f32[4,1024]{1,0:T(4,128)S(1)}, f32[256,1024]{1,0:T(8,128)}, f32[256,1024]{1,0:T(8,128)S(1)}, f32[256,1024]{1,0:...) conditional(s32[]{:T(128)} %convert_element_type.97, ...), branch_computations={%region_58.65_spmd, %region_65.76_spmd} | conditional | flops 93450412032 | bytes 474246656 | solution.py:164
  1833.9 74.5 %collective-permute-start.7 = (f32[256,1024]{1,0:T(8,128)}, f32[256,1024]{1,0:T(8,128)S(1)}, u32[]{:S(2)}, u32[]{:S(2)}) collective-permute-start(f32[256,1024]{1,0:T(8,128)} %get-tuple-element.925), channel_id=1, source_target_pairs={{0,16},{16,0},{1,17},{17,1},{2,18},{18,2},{3,19},{19,3},{4,20},{20... | collective-permute-start | bytes 3145736 | tf_op jit(solution)/shard_map/ppermute | solution.py:28
  1917.1 65.3 %reduce-scatter.11.cloned.1.call-done = f32[1,64,1024]{2,1,0:T(8,128)} async-done(((f32[1,1024,1024]{2,1,0:T(8,128)}), f32[1,64,1024]{2,1,0:T(8,128)}) %reduce-scatter.11.cloned.1.call-update) | async-done | bytes 262160 | tf_op jit(solution)/shard_map/reduce_scatter | solution.py:214
  1984.1 186.7 %reduce-scatter.17.cloned.1.call-done = f32[64,1024]{1,0:T(8,128)} async-done(((f32[2048,1024]{1,0:T(8,128)}), f32[64,1024]{1,0:T(8,128)}) %reduce-scatter.17.cloned.1.call-update) | async-done | bytes 262160 | tf_op jit(solution)/shard_map/reduce_scatter | solution.py:219
  2172.5 41.3 %all-reduce.29 = (f32[1024]{0:T(1024)S(1)}, f32[]{:T(128)}) all-reduce(f32[1024]{0:T(1024)S(1)} %get-tuple-element.1752, f32[]{:T(128)} %get-tuple-element.1872), channel_id=1, replica_groups=mesh['section'=2,'dp'=16] {'section','dp'}, use_global_device_ids=true, to_apply=%region_127.128 | all-reduce | flops 1025 | bytes 8200 | tf_op jit(solution)/shard_map/psum | solution.py:288
  2216.7 44.5 %all-reduce.28 = (f32[]{:T(128)}, f32[]{:T(128)}) all-reduce(f32[]{:T(128)} %multiply_reduce_fusion.30, f32[]{:T(128)} %multiply_reduce_fusion.31), channel_id=1, replica_groups=mesh['section'=2,'dp'=16] {'section','dp'}, use_global_device_ids=true, to_apply=%region_133.134 | all-reduce | flops 2 | bytes 16 | tf_op jit(solution)/shard_map/psum | solution.py:292
  2264.4 119.7 %reduce-scatter.9.cloned.1.call-done = f32[1,64,3072]{2,1,0:T(8,128)} async-done(((f32[1,1024,3072]{2,1,0:T(8,128)}), f32[1,64,3072]{2,1,0:T(8,128)}) %reduce-scatter.9.cloned.1.call-update) | async-done | bytes 786448 | tf_op jit(solution)/shard_map/reduce_scatter | solution.py:213
  2386.5 346.4 %reduce-scatter.15.cloned.1.call-done = f32[1,256,1024]{2,1,0:T(8,128)} async-done(((f32[1,4096,1024]{2,1,0:T(8,128)}), f32[1,256,1024]{2,1,0:T(8,128)}) %reduce-scatter.15.cloned.1.call-update) | async-done | bytes 1048592 | tf_op jit(solution)/shard_map/reduce_scatter | solution.py:216
  2735.7 352.2 %reduce-scatter.13.cloned.1.call-done = f32[1,64,4096]{2,1,0:T(8,128)} async-done(((f32[1,1024,4096]{2,1,0:T(8,128)}), f32[1,64,4096]{2,1,0:T(8,128)}) %reduce-scatter.13.cloned.1.call-update) | async-done | bytes 1048592 | tf_op jit(solution)/shard_map/reduce_scatter | solution.py:215
  3090.0 65.4 %all-reduce.31 = (f32[3072]{0:T(1024)S(1)}, f32[]{:T(128)}, f32[1024]{0:T(1024)S(1)}, f32[]{:T(128)}, f32[4096]{0:T(1024)S(1)}, /*index=5*/f32[]{:T(128)}, f32[1024]{0:T(1024)S(1)}, f32[]{:T(128)}) all-reduce(f32[3072]{0:T(1024)S(1)} %get-tuple-element.1750, f32[]{:T(128)} %get-tuple-element.1880, ...), channel_id=1, replica_groups=mesh['section'=2,'dp'=16] {'dp'}, use_global_device_ids=true, to_apply=%region_87.88 | all-reduce | flops 9220 | bytes 73760 | tf_op jit(solution)/shard_map/psum | solution.py:232
  3166.2 30.9 all-reduce.30
  (576 shorter events, 1020.5 us)
Async XLA Ops:
  7.2 83.7 %all-gather.8.cloned.1.call-start = ((), (), s32[]{:S(2)}) async-start(), calls=%async_computation.7 | async-start | bytes 4456448 | tf_op jit(solution)/shard_map/all_gather | solution.py:146
  7.9 237.2 %all-gather.6.cloned.1.call-start = ((), (), s32[]{:S(2)}) async-start(), calls=%async_computation.6 | async-start | bytes 13369344 | tf_op jit(solution)/shard_map/all_gather | solution.py:145
  8.7 316.9 %all-gather.14.cloned.1.call-start = ((), (), s32[]{:S(2)}) async-start(), calls=%async_computation.10 | async-start | bytes 8650752 | tf_op jit(solution)/shard_map/all_gather | solution.py:151
  9.4 508.1 %all-gather.10.cloned.1.call-start = ((), (), s32[]{:S(2)}) async-start(), calls=%async_computation.8 | async-start | bytes 17825792 | tf_op jit(solution)/shard_map/all_gather | solution.py:147
  10.0 700.0 %all-gather.12.cloned.1.call-start = ((), (), s32[]{:S(2)}) async-start(), calls=%async_computation.9 | async-start | bytes 17825792 | tf_op jit(solution)/shard_map/all_gather | solution.py:148
  10.6 1904.9 %reduce-scatter.19.cloned.1.call-start = ((), (), s32[]{:S(2)}) async-start(), calls=%async_computation.16 | async-start | bytes 557056
  278.7 46.8 %collective-permute-start = (f32[256,1024]{1,0:T(8,128)}, f32[256,1024]{1,0:T(8,128)}, u32[]{:S(2)}, u32[]{:S(2)}) collective-permute-start(f32[256,1024]{1,0:T(8,128)} %get-tuple-element.756), channel_id=1, source_target_pairs={{0,16},{16,0},{1,17},{17,1},{2,18},{18,2},{3,19},{19,3},{4,20},{20... | collective-permute-start | bytes 3145736 | tf_op jit(solution)/shard_map/ppermute | solution.py:28
  872.8 2.9 collective-permute-start.1
  1025.6 2.7 collective-permute-start.2
  1080.7 137.7 %collective-permute-start.3 = (f32[256,1024]{1,0:T(8,128)}, f32[256,1024]{1,0:T(8,128)}, u32[]{:S(2)}, u32[]{:S(2)}) collective-permute-start(f32[256,1024]{1,0:T(8,128)} %get-tuple-element.786), channel_id=1, source_target_pairs={{0,16},{16,0},{1,17},{17,1},{2,18},{18,2},{3,19},{19,3},{4,20},{20... | collective-permute-start | bytes 3145736 | tf_op jit(solution)/shard_map/ppermute | solution.py:28
  1467.5 2.7 collective-permute-start.4
  1714.7 2.9 collective-permute-start.5
  1740.0 242.4 %reduce-scatter.11.cloned.1.call-start = ((), (), s32[]{:S(2)}) async-start(), calls=%async_computation.12 | async-start | bytes 4456448 | tf_op jit(solution)/shard_map/reduce_scatter | solution.py:214
  1748.7 422.1 %reduce-scatter.17.cloned.1.call-start = ((), (), s32[]{:S(2)}) async-start(), calls=%async_computation.15 | async-start | bytes 8650752 | tf_op jit(solution)/shard_map/reduce_scatter | solution.py:219
  1760.9 623.2 %reduce-scatter.9.cloned.1.call-start = ((), (), s32[]{:S(2)}) async-start(), calls=%async_computation.11 | async-start | bytes 13369344 | tf_op jit(solution)/shard_map/reduce_scatter | solution.py:213
  1780.0 952.9 %reduce-scatter.15.cloned.1.call-start = ((), (), s32[]{:S(2)}) async-start(), calls=%async_computation.14 | async-start | bytes 17825792 | tf_op jit(solution)/shard_map/reduce_scatter | solution.py:216
  1803.9 1284.0 %reduce-scatter.13.cloned.1.call-start = ((), (), s32[]{:S(2)}) async-start(), calls=%async_computation.13 | async-start | bytes 17825792 | tf_op jit(solution)/shard_map/reduce_scatter | solution.py:215
  1833.9 77.2 %collective-permute-start.7 = (f32[256,1024]{1,0:T(8,128)}, f32[256,1024]{1,0:T(8,128)S(1)}, u32[]{:S(2)}, u32[]{:S(2)}) collective-permute-start(f32[256,1024]{1,0:T(8,128)} %get-tuple-element.925), channel_id=1, source_target_pairs={{0,16},{16,0},{1,17},{17,1},{2,18},{18,2},{3,19},{19,3},{4,20},{20... | collective-permute-start | bytes 3145736 | tf_op jit(solution)/shard_map/ppermute | solution.py:28
  1909.2 3.3 collective-permute-start.6
  1914.0 820.5 %copy-start.151 = (f32[1,256]{1,0:T(1,128)S(1)}, f32[1,256]{1,0:T(1,128)}, u32[]{:S(2)}) copy-start(f32[1,256]{1,0:T(1,128)} %param.51) | copy-start | bytes 3076
  1914.0 1175.3 %copy-start.155 = (f32[1,64]{1,0:T(1,128)S(1)}, f32[1,64]{1,0:T(1,128)}, u32[]{:S(2)}) copy-start(f32[1,64]{1,0:T(1,128)} %param.49) | copy-start | bytes 772
  1916.3 1289.3 %copy-start.124 = (f32[1,4,64]{2,1,0:T(4,128)}, f32[1,4,64]{2,1,0:T(4,128)S(1)}, u32[]{:S(2)}) copy-start(f32[1,4,64]{2,1,0:T(4,128)S(1)} %copy.234) | copy-start | bytes 3076
  2172.5 1033.2 %copy-start.136 = (f32[64]{0:T(128)}, f32[64]{0:T(128)S(1)}, u32[]{:S(2)}) copy-start(f32[64]{0:T(128)S(1)} %get-tuple-element.1873) | copy-start | bytes 772
  2214.4 991.2 %copy-start.118 = (f32[1024]{0:T(1024)}, f32[1024]{0:T(1024)S(1)}, u32[]{:S(2)}) copy-start(f32[1024]{0:T(1024)S(1)} %multiply_add_fusion.23) | copy-start | bytes 12292
  (145 other events, 9370.6 us)
Sparse Core Ops, SparseCore 0:
  10.8 80.0 all-gather.7
  93.7 151.3 all-gather.5
  248.0 77.4 all-gather.13
  328.2 189.3 all-gather.9
  520.2 189.7 all-gather.11
  1740.1 137.2 reduce-scatter.18
  1880.4 101.9 reduce-scatter.10
  1985.3 185.3 reduce-scatter.16
  2177.9 206.0 reduce-scatter.8
  2386.7 346.1 reduce-scatter.14
  2735.8 351.9 reduce-scatter.12
where the time goes:
time: 3250 us; the launch traced here: 3220 us
  waiting for transfers between devices  1660 us (51%)
  matrix products  541 us (17%)
  local copies, waits for them, and re-layouts  258 us (8%)
  starting transfers between devices  254 us (8%)
  blocking collectives  223 us (7%)
  other arithmetic  194 us (6%)
  loops' own time  63.5 us (2%)
    reduce_scatter x1, waiting for transfers between devices, on_device(): lax.psum_scatter(gradients[2][None], 'dp', scatter_dimension=1, tiled=True)  352 us
    reduce_scatter x1, waiting for transfers between devices, on_device(): lax.psum_scatter(gradients[3][None], 'dp', scatter_dimension=1, tiled=True)  346 us
    ppermute x8, starting transfers between devices, from_partner(): return lax.ppermute(block, axis, route)  253 us
    all_gather x1, waiting for transfers between devices, on_device(): lax.all_gather(ffn_down, 'dp', axis=1, tiled=True)  192 us
    all_gather x1, waiting for transfers between devices, on_device(): lax.all_gather(ffn_up, 'dp', axis=1, tiled=True)  192 us
    reduce_scatter x1, waiting for transfers between devices, on_device(): lax.psum_scatter(gradients[5], ('section', 'dp'), scatter_dimension=0, ti...  187 us
    all_gather x1, waiting for transfers between devices, on_device(): lax.all_gather(attn_in, 'dp', axis=1, tiled=True)  154 us
    dot_general x6, matrix products, feed_forward(): jnp.dot(normed, w_up, precision=HIGH)  132 us
  transfers between devices with their start and end apart: 19, of which 16 were waited for; matrix products, arithmetic and copies ran while one was open for 5% of the time, Pallas kernels for 0%

commit v1 on v0

v1 whole, which is shorter than its diff:
```python
from functools import partial

import jax
import jax.numpy as jnp
from jax import lax
from jax.sharding import PartitionSpec as P

HEADS = 16
STEP = 10


EPS = 1e-05
TINY = 1e-30
CLIP = 1.0
RHO = 0.5
FLOOR = 0.001
MASKED = -1e30
PRECISE = lax.Precision.HIGH
DECAY = 1.0 - STEP ** (-0.8)
NEAR = 4
PAD = 128


def place():
    me = lax.axis_index("dp")
    return me // NEAR, (me // 2) % 2, me % 2


def swap_core(block):
    return lax.ppermute(block, "section", [(0, 1), (1, 0)])


def swap_dp(block, mask):
    return lax.ppermute(block, "dp", [(i, i ^ mask) for i in range(lax.axis_size("dp"))])


def swap_split(block, mask_zero, mask_one):
    count = lax.axis_size("dp")
    masks = (mask_zero, mask_one)
    route = [(s * count + i, s * count + (i ^ masks[s])) for s in range(2) for i in range(count)]
    return lax.ppermute(block, ("section", "dp"), route)


class Lane:
    def __init__(self, depth):
        self.depth = depth
        self.given = []

    def send(self, block, move):
        if len(self.given) >= self.depth:
            block, _ = lax.optimization_barrier((block, self.given[-self.depth]))
        out = move(block)
        self.given.append(out)
        return out


def far_groups(count):
    return [[k * NEAR + low for k in range(count // NEAR)] for low in range(NEAR)]


def gather_shards(shard, lanes):
    count = lax.axis_size("dp")
    far = count // NEAR
    z, y, x = place()
    first = lax.axis_index("section") == 0
    if far > 4:
        column = lax.all_gather(shard, "dp", axis_index_groups=far_groups(count))
    else:
        column = jnp.zeros((far,) + shard.shape, shard.dtype)
        column = lax.dynamic_update_slice(column, shard[None], (z, 0, 0))
        found = lanes["z"].send(
            shard, lambda block: tuple(swap_dp(block, NEAR * k) for k in range(1, far))
        )
        for k in range(1, far):
            column = lax.dynamic_update_slice(column, found[k - 1][None], (z ^ k, 0, 0))
    from_x, from_y = lanes["xy"].send(column, lambda block: (swap_dp(block, 1), swap_dp(block, 2)))
    from_both = lanes["d"].send(
        jnp.where(first, from_x, from_y), lambda block: swap_split(block, 2, 1)
    )
    return (column, from_x, from_y, from_both)


def assemble(parts, low, high):
    z, y, x = place()
    column, from_x, from_y, from_both = [part[:, :, low:high] for part in parts]
    far, rows, width = column.shape
    whole = jnp.zeros((far, 2, 2, rows, width), column.dtype)
    whole = lax.dynamic_update_slice(whole, column[:, None, None], (0, y, x, 0, 0))
    whole = lax.dynamic_update_slice(whole, from_x[:, None, None], (0, y, 1 - x, 0, 0))
    whole = lax.dynamic_update_slice(whole, from_y[:, None, None], (0, 1 - y, x, 0, 0))
    whole = lax.dynamic_update_slice(whole, from_both[:, None, None], (0, 1 - y, 1 - x, 0, 0))
    own = whole.reshape(far * NEAR * rows, width)
    return (own, swap_core(own))


def combine(own, other, lanes):
    return own + lanes["c"].send(other, swap_core)


def spread(summed, lanes):
    count = lax.axis_size("dp")
    far = count // NEAR
    z, y, x = place()
    first = lax.axis_index("section") == 0
    rows, width = summed.shape[0] // count, summed.shape[1]
    blocks = summed.reshape(far, 2, 2, rows, width)

    def take(a, b):
        return lax.dynamic_slice(blocks, (0, a, b, 0, 0), (far, 1, 1, rows, width))[:, 0, 0]

    corner = lanes["d"].send(take(1 - y, 1 - x), lambda block: swap_split(block, 1, 2))
    to_x = take(y, 1 - x) + jnp.where(first, 0.0, corner)
    to_y = take(1 - y, x) + jnp.where(first, corner, 0.0)
    from_x, from_y = lanes["xy"].send(
        (to_x, to_y), lambda pair: (swap_dp(pair[0], 1), swap_dp(pair[1], 2))
    )
    column = take(y, x) + from_x + from_y
    if far > 4:
        return lax.psum_scatter(column, "dp", axis_index_groups=far_groups(count))

    def pick(k):
        return lax.dynamic_index_in_dim(column, z ^ k, 0, keepdims=False)

    found = lanes["z"].send(
        tuple(pick(k) for k in range(1, far)),
        lambda parts: tuple(swap_dp(part, NEAR * (k + 1)) for k, part in enumerate(parts)),
    )
    total = pick(0)
    for part in found:
        total = total + part
    return total


def hold(first, *rest):
    return lax.optimization_barrier((first, rest))[0]


def total_dp(values):
    mask = 1
    while mask < lax.axis_size("dp"):
        values = values + swap_dp(values, mask)
        mask *= 2
    return values


def by_layer(own, other, axis):
    first = lax.axis_index("section") == 0
    return jnp.where(
        first, jnp.concatenate([own, other], axis), jnp.concatenate([other, own], axis)
    )


def halves(block):
    half = block.shape[1] // 2
    section = lax.axis_index("section")
    own = lax.dynamic_slice_in_dim(block, section * half, half, 1)
    other = lax.dynamic_slice_in_dim(block, (1 - section) * half, half, 1)
    return (own, other)


def dot(left, right):
    return jnp.dot(left, right, precision=PRECISE)


def dot_t(left, right):
    return lax.dot_general(left, right, (((1,), (1,)), ((), ())), precision=PRECISE)


def t_dot(left, right):
    return lax.dot_general(left, right, (((0,), (0,)), ((), ())), precision=PRECISE)


def normalise(stream):
    centered = stream - jnp.mean(stream, axis=-1, keepdims=True)
    spread = jnp.mean(centered * centered, axis=-1, keepdims=True)
    inverse = lax.rsqrt(spread + EPS)
    return (centered * inverse, inverse)


def norm_backward(grad, unit, inverse, gain):
    scaled = grad * gain
    back = scaled - jnp.mean(scaled, axis=-1, keepdims=True)
    back = back - unit * jnp.mean(scaled * unit, axis=-1, keepdims=True)
    return (inverse * back, jnp.sum(grad * unit, axis=0), jnp.sum(grad, axis=0))


def heads_attention(projected, first_head, length, head_width):
    frame_count = projected.shape[0]
    head_count = projected.shape[1] // (3 * head_width)
    split = projected.reshape(frame_count, 3, head_count, head_width)
    scores = jnp.einsum("qhd,khd->hqk", split[:, 0], split[:, 1], precision=PRECISE)
    scores = scores * head_width ** (-0.5)
    positions = jnp.arange(frame_count)
    distance = jnp.abs(positions[:, None] - positions[None, :]).astype(jnp.float32)
    heads = (first_head + jnp.arange(head_count)).astype(jnp.float32)
    slopes = 2.0 ** (-8.0 * (heads + 1.0) / HEADS)
    scores = scores - slopes[:, None, None] * distance[None]
    scores = jnp.where((positions < length)[None, None, :], scores, MASKED)
    weighted = jnp.exp(scores - jnp.max(scores, axis=-1, keepdims=True))
    probability = weighted / jnp.sum(weighted, axis=-1, keepdims=True)
    context = jnp.einsum("hqk,khd->qhd", probability, split[:, 2], precision=PRECISE)
    return context.reshape(frame_count, head_count * head_width)


def attention_forward(stream, gain, shift, weights, length):
    in_own, in_other, out_own, out_other = weights
    section = lax.axis_index("section")
    unit, inverse = normalise(stream)
    normed = unit * gain + shift
    head_width = stream.shape[1] // HEADS
    half = HEADS // 2
    contexts = []
    pulls = []
    for w_in, first_head in ((in_own, section * half), (in_other, (1 - section) * half)):
        attend = partial(
            heads_attention, first_head=first_head, length=length, head_width=head_width
        )
        context, pull = jax.vjp(attend, dot(normed, w_in))
        contexts.append(context)
        pulls.append(pull)
    context = by_layer(contexts[0], contexts[1], 1)
    out = stream + by_layer(dot(context, out_own), dot(context, out_other), 1)
    return (out, (unit, inverse, gain, normed, context, pulls))


def attention_backward(grad, saved, weights, lanes):
    in_own, in_other, out_own, out_other = weights
    unit, inverse, gain, normed, context, pulls = saved
    grad_own, grad_other = halves(grad)
    out_grad = combine(t_dot(context, grad_own), t_dot(context, grad_other), lanes)
    context_grad = dot_t(grad_own, out_own) + dot_t(grad_other, out_other)
    back = [pull(part)[0] for pull, part in zip(pulls, halves(context_grad))]
    in_other_grad = t_dot(normed, back[1])
    in_grad = combine(t_dot(normed, back[0]), in_other_grad, lanes)
    back[0] = hold(back[0], in_other_grad)
    normed_grad = dot_t(back[0], in_own) + dot_t(back[1], in_other)
    stream_grad, gain_grad, shift_grad = norm_backward(normed_grad, unit, inverse, gain)
    grad = hold(grad + stream_grad, in_grad, out_grad)
    return (grad, spread(out_grad, lanes), spread(in_grad, lanes), gain_grad, shift_grad)


def feed_forward(stream, gain, shift, weights):
    up_own, up_other, down_own, down_other = weights
    unit, inverse = normalise(stream)
    normed = unit * gain + shift
    inner = (dot(normed, up_own), dot(normed, up_other))
    hidden = [jax.nn.gelu(part, approximate=False) for part in inner]
    out = stream + dot(hidden[0], down_own) + dot(hidden[1], down_other)
    return (out, (unit, inverse, gain, normed, inner, hidden))


def gelu_slope(value):
    bell = jnp.exp(-0.5 * value * value) * 0.3989422804014327
    return 0.5 * (1.0 + lax.erf(value * 0.7071067811865476)) + value * bell


def feed_backward(grad, saved, weights, lanes):
    up_own, up_other, down_own, down_other = weights
    unit, inverse, gain, normed, inner, hidden = saved
    down_other_grad = t_dot(hidden[1], grad)
    down_grad = combine(t_dot(hidden[0], grad), down_other_grad, lanes)
    held = hold(grad, down_other_grad)
    back_other = dot_t(held, down_other) * gelu_slope(inner[1])
    up_other_grad = t_dot(normed, back_other)
    held = hold(held, up_other_grad)
    back_own = dot_t(held, down_own) * gelu_slope(inner[0])
    up_grad = combine(t_dot(normed, back_own), up_other_grad, lanes)
    normed_grad = dot_t(back_own, up_own) + dot_t(back_other, up_other)
    stream_grad, gain_grad, shift_grad = norm_backward(normed_grad, unit, inverse, gain)
    grad = hold(grad + stream_grad, down_grad, up_grad)
    return (grad, spread(down_grad, lanes), spread(up_grad, lanes), gain_grad, shift_grad)


def local_moments(grad, rows_old, weight):
    squared = grad * grad + TINY
    rows_new = DECAY * rows_old + (1.0 - DECAY) * jnp.mean(squared, axis=1)
    scaled = jnp.sum(grad * grad / rows_new[:, None], axis=0)
    pair = jnp.stack([jnp.sum(rows_new), jnp.sum(weight * weight)])
    return (rows_new, [jnp.sum(squared, axis=0), scaled, pair])


def finish(grad, weight, rows_new, cols_old, totals, total_rows):
    column_total, scaled_total, pair = totals
    cols_new = DECAY * cols_old + (1.0 - DECAY) * (column_total / total_rows)
    rows_mean = pair[0] / total_rows
    second = rows_new[:, None] * cols_new[None, :] / rows_mean
    update = grad * lax.rsqrt(second)
    count = total_rows * grad.shape[1]
    ratio = jnp.sqrt(rows_mean * jnp.sum(scaled_total / cols_new) / count) / CLIP
    scale = jnp.maximum(jnp.sqrt(pair[1] / count), FLOOR)
    return (cols_new, weight - RHO * scale * (update / jnp.maximum(ratio, 1.0)))


def on_device(
    frames,
    cotangent,
    lengths,
    attn_in,
    attn_out,
    ffn_up,
    ffn_down,
    norm_params,
    skip_proj,
    in_rows,
    in_cols,
    out_rows,
    out_cols,
    up_rows,
    up_cols,
    down_rows,
    down_cols,
    skip_rows,
    skip_cols,
    norm_moment,
):
    section = lax.axis_index("section")
    me = lax.axis_index("dp")
    data_size = lax.axis_size("dp")
    first = section == 0
    frame_count, model_width = frames.shape[2], frames.shape[3]
    width = model_width // 2
    share = attn_in.shape[1]
    ffn_share = ffn_down.shape[1]
    source = lax.dynamic_index_in_dim(frames, section, 0, keepdims=False)[0]
    length = lax.dynamic_index_in_dim(lengths, section, 0, keepdims=False)[0]
    valid_rows = (jnp.arange(frame_count) < length).astype(jnp.float32)[:, None]
    outer = lax.dynamic_index_in_dim(cotangent, section, 0, keepdims=False)[0] * valid_rows

    def attn_half(s):
        heads_in = attn_in[0].reshape(share, 3, 2, width)
        inner = lax.dynamic_index_in_dim(heads_in, s, 2, keepdims=False).reshape(share, 3 * width)
        return jnp.concatenate(
            [inner, lax.dynamic_slice_in_dim(attn_out[0], s * width, width, 1)], 1
        )

    def up_half(s):
        hidden_cols = ffn_up[0].reshape(share, data_size, 2, ffn_share // 2)
        return lax.dynamic_index_in_dim(hidden_cols, s, 2, keepdims=False).reshape(share, -1)

    def down_half(s):
        return lax.dynamic_slice_in_dim(ffn_down[0], s * (ffn_share // 2), ffn_share // 2, 0)

    def by_owner(half):
        kept = half(section)
        given = swap_core(half(1 - section))
        return (jnp.where(first, kept, given), jnp.where(first, given, kept))

    attn_zero, attn_one = by_owner(attn_half)
    up_zero, up_one = by_owner(up_half)
    down_zero, down_one = by_owner(down_half)
    norm_shard = jnp.pad(norm_params[0].T, ((0, 0), (0, PAD - norm_params.shape[1])))

    lanes = {"z": Lane(1), "xy": Lane(1), "d": Lane(1)}
    parts = gather_shards(jnp.concatenate([attn_zero, norm_shard], 1), lanes)
    attn_zero_full = assemble(parts, 0, 3 * width) + assemble(parts, 3 * width, 4 * width)
    norms = [full[:, :4].T for full in assemble(parts, 4 * width, 4 * width + PAD)]
    norm_zero = jnp.where(first, norms[0], norms[1])
    norm_one = jnp.where(first, norms[1], norms[0])
    ffn_one_full = assemble(gather_shards(up_one, lanes), 0, up_one.shape[1]) + assemble(
        gather_shards(down_one, lanes), 0, model_width
    )
    skip_full = assemble(gather_shards(skip_proj, lanes), 0, model_width)
    parts = gather_shards(attn_one, lanes)
    attn_one_full = assemble(parts, 0, 3 * width) + assemble(parts, 3 * width, 4 * width)
    ffn_zero_full = assemble(gather_shards(up_zero, lanes), 0, up_zero.shape[1]) + assemble(
        gather_shards(down_zero, lanes), 0, model_width
    )

    after_attn, saved_a0 = attention_forward(
        source, norm_zero[0], norm_zero[1], attn_zero_full, length
    )
    twelve, saved_f1 = feed_forward(after_attn, norm_one[2], norm_one[3], ffn_one_full)
    joined_own = jnp.where(first, twelve, source)
    joined_other = jnp.where(first, source, twelve)
    joined = dot(joined_own, skip_full[0]) + dot(joined_other, skip_full[1])
    middle, saved_a1 = attention_forward(
        joined, norm_one[0], norm_one[1], attn_one_full, length
    )
    thirteen, saved_f0 = feed_forward(middle, norm_zero[2], norm_zero[3], ffn_zero_full)

    lanes = {"z": Lane(1), "xy": Lane(1), "d": Lane(1), "c": Lane(2)}
    grad, down_zero_s, up_zero_s, g02, g03 = feed_backward(outer, saved_f0, ffn_zero_full, lanes)
    grad, out_one_s, in_one_s, g10, g11 = attention_backward(
        grad, saved_a1, attn_one_full, lanes
    )
    skip_sum = combine(t_dot(joined_own, grad), t_dot(joined_other, grad), lanes)
    skip_grad = spread(skip_sum, lanes)
    back_own = dot_t(grad, skip_full[0])
    back_other = dot_t(grad, skip_full[1])
    frames_grad = jnp.where(first, back_other, back_own)
    grad = hold(jnp.where(first, back_own, back_other), skip_sum)
    grad, down_one_s, up_one_s, g12, g13 = feed_backward(grad, saved_f1, ffn_one_full, lanes)
    after_attn_grad = grad
    grad, out_zero_s, in_zero_s, g00, g01 = attention_backward(
        grad, saved_a0, attn_zero_full, lanes
    )
    frames_grad = frames_grad + grad

    def to_owner(zero, one):
        kept = jnp.where(first, zero, one)
        given = swap_core(jnp.where(first, one, zero))
        return (jnp.where(first, kept, given), jnp.where(first, given, kept))

    def regroup(pair, groups):
        parts = [part.reshape(part.shape[0], groups, -1) for part in pair]
        return jnp.stack(parts, 2).reshape(parts[0].shape[0], -1)

    shares = [
        regroup(to_owner(in_zero_s, in_one_s), 3),
        regroup(to_owner(out_zero_s, out_one_s), 1),
        regroup(to_owner(up_zero_s, up_one_s), data_size),
        jnp.concatenate(to_owner(down_zero_s, down_one_s), 0),
    ]

    norm_grads = total_dp(jnp.stack([g00, g01, g02, g03, g10, g11, g12, g13]))
    norm_grads = (norm_grads + swap_core(norm_grads)).reshape(2, 4, model_width)
    norm_share = lax.dynamic_slice(norm_grads, (section, 0, me * share), (1, 4, share))[0]

    current = [attn_in[0], attn_out[0], ffn_up[0], ffn_down[0]]
    rows_old = [in_rows[0], out_rows[0], up_rows[0], down_rows[0]]
    cols_old = [in_cols[0], out_cols[0], up_cols[0], down_cols[0]]
    moments = [local_moments(g, r, w) for g, r, w in zip(shares, rows_old, current)]
    skip_rows_new, skip_local = local_moments(skip_grad, skip_rows, skip_proj)
    norm_moment_new = DECAY * norm_moment[0] + (1.0 - DECAY) * (norm_share * norm_share + TINY)
    norm_raw = norm_share * lax.rsqrt(norm_moment_new)
    norm_sums = [
        jnp.sum(norm_raw * norm_raw, axis=-1),
        jnp.sum(norm_params[0] * norm_params[0], axis=-1),
    ]
    vectors = skip_local + [v for _, local in moments for v in local] + norm_sums
    sizes = [v.shape[0] for v in vectors]
    packed = jnp.concatenate(vectors)
    packed = total_dp(jnp.pad(packed, (0, -packed.shape[0] % PAD)))
    skip_size = sum(sizes[:3])
    skip_totals = packed[:skip_size] + swap_core(packed[:skip_size])
    offsets = [sum(sizes[:k]) for k in range(len(sizes))]
    totals = [packed[at : at + size] for at, size in zip(offsets, sizes)]
    updated = [
        finish(
            shares[k],
            current[k],
            moments[k][0],
            cols_old[k],
            totals[3 + 3 * k : 6 + 3 * k],
            shares[k].shape[0] * data_size,
        )
        for k in range(4)
    ]
    skip_cols_new, skip_new = finish(
        skip_grad,
        skip_proj,
        skip_rows_new,
        skip_cols,
        [skip_totals[at : at + size] for at, size in zip(offsets[:3], sizes[:3])],
        skip_grad.shape[0] * data_size * 2,
    )
    norm_ratio = jnp.sqrt(totals[15] / model_width) / CLIP
    norm_scale = jnp.maximum(jnp.sqrt(totals[16] / model_width), FLOOR)
    norms_new = norm_params[0] - RHO * norm_scale[:, None] * (
        norm_raw / jnp.maximum(norm_ratio, 1.0)[:, None]
    )

    def both_micro(zero, one):
        kept = jnp.where(first, zero, one)
        given = swap_core(jnp.where(first, one, zero))
        pair = jnp.where(first, jnp.stack([kept, given]), jnp.stack([given, kept]))
        return pair[None, :, None]

    layer_outputs = both_micro(thirteen, twelve)
    input_grads = both_micro(frames_grad, after_attn_grad)
    return (
        layer_outputs,
        input_grads,
        shares[0][None],
        moments[0][0][None],
        updated[0][0][None],
        updated[0][1][None],
        shares[1][None],
        moments[1][0][None],
        updated[1][0][None],
        updated[1][1][None],
        shares[2][None],
        moments[2][0][None],
        updated[2][0][None],
        updated[2][1][None],
        shares[3][None],
        moments[3][0][None],
        updated[3][0][None],
        updated[3][1][None],
        skip_grad,
        skip_rows_new,
        skip_cols_new,
        skip_new,
        norm_share[None],
        norm_moment_new[None],
        norms_new[None],
    )


def solution(mesh):
    return jax.shard_map(
        on_device,
        mesh=mesh,
        in_specs=(
            P(None, "dp", None, None),
            P(None, "dp", None, None),
            P(None, "dp"),
            P("section", "dp", None),
            P("section", "dp", None),
            P("section", "dp", None),
            P("section", "dp", None),
            P("section", None, "dp"),
            P(("section", "dp"), None),
            P("section", "dp"),
            P("section", None),
            P("section", "dp"),
            P("section", None),
            P("section", "dp"),
            P("section", None),
            P("section", "dp"),
            P("section", None),
            P(("section", "dp")),
            P(),
            P("section", None, "dp"),
        ),
        out_specs=(
            P("section", None, "dp", None, None),
            P("section", None, "dp", None, None),
            P("section", "dp", None),
            P("section", "dp"),
            P("section", None),
            P("section", "dp", None),
            P("section", "dp", None),
            P("section", "dp"),
            P("section", None),
            P("section", "dp", None),
            P("section", "dp", None),
            P("section", "dp"),
            P("section", None),
            P("section", "dp", None),
            P("section", "dp", None),
            P("section", "dp"),
            P("section", None),
            P("section", "dp", None),
            P(("section", "dp"), None),
            P(("section", "dp")),
            P(),
            P(("section", "dp"), None),
            P("section", None, "dp"),
            P("section", None, "dp"),
            P("section", None, "dp"),
        ),
        check_vma=False,
    )
```

time: 3250 us -> 1580 us (0.49)
  waiting for transfers between devices: 1660 us -> 534 us
  blocking collectives: 223 us -> 0 us
  matrix products: 541 us -> 374 us
  other arithmetic: 194 us -> 128 us
  loops' own time: 63.5 us -> 0 us
  starting transfers between devices: 254 us -> 308 us
  local copies, waits for them, and re-layouts: 258 us -> 214 us
    reduce_scatter x5 -> x0, waiting for transfers between devices: 1070 us -> none  [the longest x1 352 us: on_device(): lax.psum_scatter(gradients[2][None], 'dp', scatter_dimension=1, tiled=True)]
    all_gather x5 -> x0, waiting for transfers between devices: 576 us -> none  [the longest x1 192 us: on_device(): lax.all_gather(ffn_down, 'dp', axis=1, tiled=True)]
    ppermute x8 -> x134, waiting for transfers between devices: 9.99 us -> 534 us  [the longest x88 420 us: swap_dp(): lax.ppermute(block, 'dp', [(i, i ^ mask) for i in range(lax.axis_size('dp...]
    psum x4 -> x0, blocking collectives: 182 us -> none  [the longest x1 65.4 us: on_device(): lax.psum((moments[0][1], row_sums[0], weight_sums[0], moments[1][1], row_...]
    dot_general x42 -> x78, matrix products: 541 us -> 374 us  [the longest x18 119 us: dot(): return jnp.dot(left, right, precision=PRECISE)]
    cond x107 -> x0, local copies, waits for them, and re-layouts: 135 us -> none
    dynamic_update_slice x0 -> x62, local copies, waits for them, and re-layouts: none -> 81.5 us  [the longest x10 18.6 us: assemble(): lax.dynamic_update_slice(whole, from_both[:, None, None], (0, 1 - y, 1 -...]
    broadcast_in_dim x7 -> x1, other arithmetic: 78.5 us -> 1.06 us  [on_device(): shares[3][None]]
  transfers between devices with their start and end apart: 19 -> 134, of which waited for: 16 -> 55; matrix products, arithmetic and copies ran while one was open for 5% -> 42% of each run, Pallas kernels for 0% -> 0%
where the time goes in v1:
time: 1580 us; the launch traced here: 1570 us
  waiting for transfers between devices  534 us (34%)
  matrix products  374 us (24%)
  starting transfers between devices  308 us (19%)
  local copies, waits for them, and re-layouts  214 us (14%)
  other arithmetic  128 us (8%)
    ppermute x88, waiting for transfers between devices, swap_dp(): lax.ppermute(block, 'dp', [(i, i ^ mask) for i in range(lax.axis_size('dp...  420 us
    ppermute x88, starting transfers between devices, swap_dp(): lax.ppermute(block, 'dp', [(i, i ^ mask) for i in range(lax.axis_size('dp...  208 us
    dot_general x18, matrix products, dot(): return jnp.dot(left, right, precision=PRECISE)  119 us
    ppermute x16, waiting for transfers between devices, swap_split(): return lax.ppermute(block, ('section', 'dp'), route)  113 us
    dot_general x18, matrix products, t_dot(): lax.dot_general(left, right, (((0,), (0,)), ((), ())), precision=PRECISE)  106 us
    dot_general x18, matrix products, dot_t(): lax.dot_general(left, right, (((1,), (1,)), ((), ())), precision=PRECISE)  105 us
    ppermute x30, starting transfers between devices, swap_core(): return lax.ppermute(block, 'section', [(0, 1), (1, 0)])  87 us
    another operation x13, local copies, waits for them, and re-layouts  32 us
  transfers between devices with their start and end apart: 134, of which 55 were waited for; matrix products, arithmetic and copies ran while one was open for 42% of the time, Pallas kernels for 0%

profile of v1, /device:TPU:1, one launch (start us, length us, event | category | flops | bytes accessed | tf_op | source)
XLA Modules:
  0.0 1571.7 jit_solution(14392482900313067327)
XLA Ops:
  53.3 15.3 collective-permute-done.2
  103.1 13.8 collective-permute-done.13
  149.3 14.2 collective-permute-done.20
  217.6 15.4 collective-permute-done.35
  262.5 14.8 collective-permute-done.43
  335.3 14.3 collective-permute-start.7
  378.8 24.3 %collective-permute-done.16 = f32[4,64,2048]{2,1,0:T(8,128)} collective-permute-done((f32[4,64,2048]{2,1,0:T(8,128)}, f32[4,64,2048]{2,1,0:T(8,128)}, u32[]{:S(2)}, u32[]{:S(2)}) %collective-permute-start.16) | collective-permute-done | bytes 2097184 | tf_op jit(solution)/shard_map/ppermute | solution.py:41
  405.6 15.3 collective-permute-done.29
  439.0 16.9 %collective-permute-done.23 = f32[4,128,1024]{2,1,0:T(8,128)} collective-permute-done((f32[4,128,1024]{2,1,0:T(8,128)}, f32[4,128,1024]{2,1,0:T(8,128)}, u32[]{:S(2)}, u32[]{:S(2)}) %collective-permute-start.23) | collective-permute-done | bytes 2097184 | tf_op jit(solution)/shard_map/ppermute | solution.py:41
  455.9 15.3 collective-permute-start.24
  474.3 13.9 collective-permute-done.36
  555.4 28.1 %collective-permute-done.38 = f32[4,64,2048]{2,1,0:T(8,128)S(1)} collective-permute-done((f32[4,64,2048]{2,1,0:T(8,128)S(1)}, f32[4,64,2048]{2,1,0:T(8,128)S(1)}, u32[]{:S(2)}, u32[]{:S(2)}) %collective-permute-start.38) | collective-permute-done | bytes 2097184 | tf_op jit(solution)/shard_map/ppermute | solution.py:41
  597.2 20.3 %collective-permute-done.50 = f32[4,128,1024]{2,1,0:T(8,128)} collective-permute-done((f32[4,128,1024]{2,1,0:T(8,128)}, f32[4,128,1024]{2,1,0:T(8,128)}, u32[]{:S(2)}, u32[]{:S(2)}) %collective-permute-start.50) | collective-permute-done | bytes 2097184 | tf_op jit(solution)/shard_map/ppermute | solution.py:34
  626.5 13.6 collective-permute-done.46
  914.6 15.1 collective-permute-done.76
  1001.9 13.5 collective-permute-start.96
  1034.3 22.0 %collective-permute-done.97 = f32[64,2048]{1,0:T(8,128)} collective-permute-done((f32[64,2048]{1,0:T(8,128)}, f32[64,2048]{1,0:T(8,128)}, u32[]{:S(2)}, u32[]{:S(2)}) %collective-permute-start.97) | collective-permute-done | bytes 524320 | tf_op jit(solution)/shard_map/ppermute | solution.py:34
  1232.5 13.5 select_bitcast_fusion.1
  1257.8 14.6 collective-permute-done.85
  1316.5 13.5 collective-permute-start.123
  1347.1 34.0 %collective-permute-done.87 = f32[4,64,2048]{2,1,0:T(8,128)S(1)} collective-permute-done((f32[4,64,2048]{2,1,0:T(8,128)S(1)}, f32[4,64,2048]{2,1,0:T(8,128)S(1)}, u32[]{:S(2)}, u32[]{:S(2)}) %collective-permute-start.87) | collective-permute-done | bytes 2097184 | tf_op jit(solution)/shard_map/ppermute | solution.py:34
  1411.7 13.5 collective-permute-done.113
  1455.9 16.2 %collective-permute-done.92 = f32[4,64,1536]{2,1,0:T(8,128)S(1)} collective-permute-done((f32[4,64,1536]{2,1,0:T(8,128)S(1)}, f32[4,64,1536]{2,1,0:T(8,128)S(1)}, u32[]{:S(2)}, u32[]{:S(2)}) %collective-permute-start.92) | collective-permute-done | bytes 1572896 | tf_op jit(solution)/shard_map/ppermute | solution.py:34
  1481.5 25.8 %collective-permute-done.118 = f32[64,1536]{1,0:T(8,128)S(1)} collective-permute-done((f32[64,1536]{1,0:T(8,128)S(1)}, f32[64,1536]{1,0:T(8,128)S(1)}, u32[]{:S(2)}, u32[]{:S(2)}) %collective-permute-start.118) | collective-permute-done | bytes 393248 | tf_op jit(solution)/shard_map/ppermute | solution.py:34
  (1039 shorter events, 1140.3 us)
Async XLA Ops:
  82.9 171.4 %collective-permute-start.4 = (f32[4,64,2176]{2,1,0:T(8,128)S(1)}, f32[4,64,2176]{2,1,0:T(8,128)S(1)}, u32[]{:S(2)}, u32[]{:S(2)}) collective-permute-start(f32[4,64,2176]{2,1,0:T(8,128)S(1)} %bitcast_dynamic-update-slice_fusion.20), channel_id=1, source_target_pairs={{0,1},{1,0},{2,3},{3,2},{4,5},{5,4},{6,7},{7,6},{8,9},{9,8},{10,11... | collective-permute-start | bytes 6684680 | tf_op jit(solution)/shard_map/ppermute | solution.py:34
  84.2 170.2 %collective-permute-start.5 = (f32[4,64,2176]{2,1,0:T(8,128)S(1)}, f32[4,64,2176]{2,1,0:T(8,128)S(1)}, u32[]{:S(2)}, u32[]{:S(2)}) collective-permute-start(f32[4,64,2176]{2,1,0:T(8,128)S(1)} %bitcast_dynamic-update-slice_fusion.20), channel_id=1, source_target_pairs={{0,2},{1,3},{2,0},{3,1},{4,6},{5,7},{6,4},{7,5},{8,10},{9,11},{10,... | collective-permute-start | bytes 6684680 | tf_op jit(solution)/shard_map/ppermute | solution.py:34
  254.3 73.7 %collective-permute-start.14 = (f32[4,64,2048]{2,1,0:T(8,128)S(1)}, f32[4,64,2048]{2,1,0:T(8,128)S(1)}, u32[]{:S(2)}, u32[]{:S(2)}) collective-permute-start(f32[4,64,2048]{2,1,0:T(8,128)S(1)} %bitcast_dynamic-update-slice_fusion.40), channel_id=1, source_target_pairs={{0,1},{1,0},{2,3},{3,2},{4,5},{5,4},{6,7},{7,6},{8,9},{9,8},{10,11... | collective-permute-start | bytes 6291464 | tf_op jit(solution)/shard_map/ppermute | solution.py:34
  255.5 72.5 %collective-permute-start.15 = (f32[4,64,2048]{2,1,0:T(8,128)S(1)}, f32[4,64,2048]{2,1,0:T(8,128)S(1)}, u32[]{:S(2)}, u32[]{:S(2)}) collective-permute-start(f32[4,64,2048]{2,1,0:T(8,128)S(1)} %bitcast_dynamic-update-slice_fusion.40), channel_id=1, source_target_pairs={{0,2},{1,3},{2,0},{3,1},{4,6},{5,7},{6,4},{7,5},{8,10},{9,11},{10,... | collective-permute-start | bytes 6291464 | tf_op jit(solution)/shard_map/ppermute | solution.py:34
  335.0 68.1 %collective-permute-start.16 = (f32[4,64,2048]{2,1,0:T(8,128)}, f32[4,64,2048]{2,1,0:T(8,128)}, u32[]{:S(2)}, u32[]{:S(2)}) collective-permute-start(f32[4,64,2048]{2,1,0:T(8,128)} %broadcast_select_fusion.5), channel_id=1, source_target_pairs={{0,2},{1,3},{2,0},{3,1},{4,6},{5,7},{6,4},{7,5},{8,10},{9,11},{10,... | collective-permute-start | bytes 6291464 | tf_op jit(solution)/shard_map/ppermute | solution.py:41
  350.9 153.5 %collective-permute-start.8 = (f32[1024,1536]{1,0:T(8,128)}, f32[1024,1536]{1,0:T(8,128)}, u32[]{:S(2)}, u32[]{:S(2)}) collective-permute-start(f32[1024,1536]{1,0:T(8,128)} %bitcast.29), channel_id=1, source_target_pairs={{0,16},{16,0},{1,17},{17,1},{2,18},{18,2},{3,19},{19,3},{4,20},{20... | collective-permute-start | bytes 18874376 | tf_op jit(solution)/shard_map/ppermute | solution.py:30
  360.5 165.2 %collective-permute-start.9 = (f32[1024,512]{1,0:T(8,128)}, f32[1024,512]{1,0:T(8,128)}, u32[]{:S(2)}, u32[]{:S(2)}) collective-permute-start(f32[1024,512]{1,0:T(8,128)} %bitcast.941), channel_id=1, source_target_pairs={{0,16},{16,0},{1,17},{17,1},{2,18},{18,2},{3,19},{19,3},{4,20},{20... | collective-permute-start | bytes 6291464 | tf_op jit(solution)/shard_map/ppermute | solution.py:30
  455.9 188.5 %collective-permute-start.24 = (f32[1024,2048]{1,0:T(8,128)}, f32[1024,2048]{1,0:T(8,128)}, u32[]{:S(2)}, u32[]{:S(2)}) collective-permute-start(f32[1024,2048]{1,0:T(8,128)} %bitcast.74), channel_id=1, source_target_pairs={{0,16},{16,0},{1,17},{17,1},{2,18},{18,2},{3,19},{19,3},{4,20},{20... | collective-permute-start | bytes 25165832 | tf_op jit(solution)/shard_map/ppermute | solution.py:30
  488.2 182.6 %collective-permute-start.25 = (f32[2048,1024]{1,0:T(8,128)}, f32[2048,1024]{1,0:T(8,128)}, u32[]{:S(2)}, u32[]{:S(2)}) collective-permute-start(f32[2048,1024]{1,0:T(8,128)} %bitcast.88), channel_id=1, source_target_pairs={{0,16},{16,0},{1,17},{17,1},{2,18},{18,2},{3,19},{19,3},{4,20},{20... | collective-permute-start | bytes 25165832 | tf_op jit(solution)/shard_map/ppermute | solution.py:30
  545.2 72.4 %collective-permute-start.50 = (f32[4,128,1024]{2,1,0:T(8,128)}, f32[4,128,1024]{2,1,0:T(8,128)}, u32[]{:S(2)}, u32[]{:S(2)}) collective-permute-start(f32[4,128,1024]{2,1,0:T(8,128)} %bitcast_dynamic-update-slice_fusion.24), channel_id=1, source_target_pairs={{0,1},{1,0},{2,3},{3,2},{4,5},{5,4},{6,7},{7,6},{8,9},{9,8},{10,11... | collective-permute-start | bytes 6291464 | tf_op jit(solution)/shard_map/ppermute | solution.py:34
  547.8 73.0 %collective-permute-start.51 = (f32[4,128,1024]{2,1,0:T(8,128)}, f32[4,128,1024]{2,1,0:T(8,128)}, u32[]{:S(2)}, u32[]{:S(2)}) collective-permute-start(f32[4,128,1024]{2,1,0:T(8,128)} %bitcast_dynamic-update-slice_fusion.24), channel_id=1, source_target_pairs={{0,2},{1,3},{2,0},{3,1},{4,6},{5,7},{6,4},{7,5},{8,10},{9,11},{10,... | collective-permute-start | bytes 6291464 | tf_op jit(solution)/shard_map/ppermute | solution.py:34
  617.5 72.0 %collective-permute-start.32 = (f32[1024,1024]{1,0:T(8,128)}, f32[1024,1024]{1,0:T(8,128)S(1)}, u32[]{:S(2)}, u32[]{:S(2)}) collective-permute-start(f32[1024,1024]{1,0:T(8,128)} %bitcast.100), channel_id=1, source_target_pairs={{0,16},{16,0},{1,17},{17,1},{2,18},{18,2},{3,19},{19,3},{4,20},{20... | collective-permute-start | bytes 12582920 | tf_op jit(solution)/shard_map/ppermute | solution.py:30
  620.8 85.4 %collective-permute-start.39 = (f32[1024,1536]{1,0:T(8,128)}, f32[1024,1536]{1,0:T(8,128)}, u32[]{:S(2)}, u32[]{:S(2)}) collective-permute-start(f32[1024,1536]{1,0:T(8,128)} %bitcast.114), channel_id=1, source_target_pairs={{0,16},{16,0},{1,17},{17,1},{2,18},{18,2},{3,19},{19,3},{4,20},{20... | collective-permute-start | bytes 18874376 | tf_op jit(solution)/shard_map/ppermute | solution.py:30
  644.4 81.6 %collective-permute-start.53 = (f32[1024,2048]{1,0:T(8,128)}, f32[1024,2048]{1,0:T(8,128)}, u32[]{:S(2)}, u32[]{:S(2)}) collective-permute-start(f32[1024,2048]{1,0:T(8,128)} %bitcast.151), channel_id=1, source_target_pairs={{0,16},{16,0},{1,17},{17,1},{2,18},{18,2},{3,19},{19,3},{4,20},{20... | collective-permute-start | bytes 25165832 | tf_op jit(solution)/shard_map/ppermute | solution.py:30
  670.8 70.2 %collective-permute-start.54 = (f32[2048,1024]{1,0:T(8,128)}, f32[2048,1024]{1,0:T(8,128)}, u32[]{:S(2)}, u32[]{:S(2)}) collective-permute-start(f32[2048,1024]{1,0:T(8,128)} %bitcast.164), channel_id=1, source_target_pairs={{0,16},{16,0},{1,17},{17,1},{2,18},{18,2},{3,19},{19,3},{4,20},{20... | collective-permute-start | bytes 25165832 | tf_op jit(solution)/shard_map/ppermute | solution.py:30
  979.1 154.8 %collective-permute-start.61 = (f32[2048,1024]{1,0:T(8,128)}, f32[2048,1024]{1,0:T(8,128)}, u32[]{:S(2)}, u32[]{:S(2)}) collective-permute-start(f32[2048,1024]{1,0:T(8,128)} %fusion.353), channel_id=1, source_target_pairs={{0,16},{16,0},{1,17},{17,1},{2,18},{18,2},{3,19},{19,3},{4,20},{20... | collective-permute-start | bytes 25165832 | tf_op jit(solution)/shard_map/ppermute | solution.py:30
  998.9 147.4 %collective-permute-start.62 = (f32[1024,2048]{1,0:T(8,128)}, f32[1024,2048]{1,0:T(8,128)}, u32[]{:S(2)}, u32[]{:S(2)}) collective-permute-start(f32[1024,2048]{1,0:T(8,128)} %fusion.158), channel_id=1, source_target_pairs={{0,16},{16,0},{1,17},{17,1},{2,18},{18,2},{3,19},{19,3},{4,20},{20... | collective-permute-start | bytes 25165832 | tf_op jit(solution)/shard_map/ppermute | solution.py:30
  1089.1 124.5 %collective-permute-start.102 = (f32[64,1536]{1,0:T(8,128)}, f32[64,1536]{1,0:T(8,128)S(1)}, u32[]{:S(2)}, u32[]{:S(2)}) collective-permute-start(f32[64,1536]{1,0:T(8,128)} %get-tuple-element.175), channel_id=1, source_target_pairs={{0,4},{1,5},{2,6},{3,7},{4,0},{5,1},{6,2},{7,3},{8,12},{9,13},{10,... | collective-permute-start | bytes 1179656 | tf_op jit(solution)/shard_map/ppermute | solution.py:34
  1130.3 83.3 %collective-permute-start.103 = (f32[64,1536]{1,0:T(8,128)}, f32[64,1536]{1,0:T(8,128)}, u32[]{:S(2)}, u32[]{:S(2)}) collective-permute-start(f32[64,1536]{1,0:T(8,128)} %get-tuple-element.176), channel_id=1, source_target_pairs={{0,8},{1,9},{2,10},{3,11},{4,12},{5,13},{6,14},{7,15},{8,0},{9,1},... | collective-permute-start | bytes 1179656 | tf_op jit(solution)/shard_map/ppermute | solution.py:34
  1131.5 82.1 %collective-permute-start.104 = (f32[64,1536]{1,0:T(8,128)}, f32[64,1536]{1,0:T(8,128)}, u32[]{:S(2)}, u32[]{:S(2)}) collective-permute-start(f32[64,1536]{1,0:T(8,128)} %get-tuple-element.177), channel_id=1, source_target_pairs={{0,12},{1,13},{2,14},{3,15},{4,8},{5,9},{6,10},{7,11},{8,4},{9,5},... | collective-permute-start | bytes 1179656 | tf_op jit(solution)/shard_map/ppermute | solution.py:34
  1221.1 116.2 %collective-permute-start.63 = (f32[1024,1536]{1,0:T(8,128)}, f32[1024,1536]{1,0:T(8,128)}, u32[]{:S(2)}, u32[]{:S(2)}) collective-permute-start(f32[1024,1536]{1,0:T(8,128)} %fusion.123), channel_id=1, source_target_pairs={{0,16},{16,0},{1,17},{17,1},{2,18},{18,2},{3,19},{19,3},{4,20},{20... | collective-permute-start | bytes 18874376 | tf_op jit(solution)/shard_map/ppermute | solution.py:30
  1345.6 94.0 %collective-permute-start.74 = (f32[4,64,1536]{2,1,0:T(8,128)S(1)}, f32[4,64,1536]{2,1,0:T(8,128)S(1)}, u32[]{:S(2)}, u32[]{:S(2)}) collective-permute-start(f32[4,64,1536]{2,1,0:T(8,128)S(1)} %dynamic-slice_bitcast_fusion.5), channel_id=1, source_target_pairs={{0,1},{1,0},{2,3},{3,2},{4,5},{5,4},{6,7},{7,6},{8,9},{9,8},{10,11... | collective-permute-start | bytes 4718600 | tf_op jit(solution)/shard_map/ppermute | solution.py:41
  1443.6 80.7 %collective-permute-start.55 = (f32[256,1024]{1,0:T(8,128)}, f32[256,1024]{1,0:T(8,128)}, u32[]{:S(2)}, u32[]{:S(2)}) collective-permute-start(f32[256,1024]{1,0:T(8,128)} %get-tuple-element.338), channel_id=1, source_target_pairs={{0,16},{16,0},{1,17},{17,1},{2,18},{18,2},{3,19},{19,3},{4,20},{20... | collective-permute-start | bytes 3145736 | tf_op jit(solution)/shard_map/ppermute | solution.py:30
  1454.2 78.8 %collective-permute-start.65 = (f32[256,1024]{1,0:T(8,128)}, f32[256,1024]{1,0:T(8,128)}, u32[]{:S(2)}, u32[]{:S(2)}) collective-permute-start(f32[256,1024]{1,0:T(8,128)} %get-tuple-element.316), channel_id=1, source_target_pairs={{0,16},{16,0},{1,17},{17,1},{2,18},{18,2},{3,19},{19,3},{4,20},{20... | collective-permute-start | bytes 3145736 | tf_op jit(solution)/shard_map/ppermute | solution.py:30
  (317 other events, 7491.9 us)

commit v2 on v1

v2 whole, which is shorter than its diff:
```python
import math
from functools import partial

import jax
import jax.numpy as jnp
from jax import lax
from jax.experimental import pallas as pl
from jax.experimental.pallas import tpu as pltpu
from jax.sharding import PartitionSpec as P

HEADS = 16
STEP = 10


EPS = 1e-05
TINY = 1e-30
CLIP = 1.0
RHO = 0.5
FLOOR = 0.001
MASKED = -1e30
DECAY = 1.0 - STEP ** (-0.8)
PAD = 128
DIRECT = 16


def swap_core(block):
    return lax.ppermute(block, "section", [(0, 1), (1, 0)])


def swap_dp(block, mask):
    return lax.ppermute(block, "dp", [(i, i ^ mask) for i in range(lax.axis_size("dp"))])


def swap_split(block, mask_zero, mask_one):
    count = lax.axis_size("dp")
    masks = (mask_zero, mask_one)
    route = [(s * count + i, s * count + (i ^ masks[s])) for s in range(2) for i in range(count)]
    return lax.ppermute(block, ("section", "dp"), route)


def hold(first, *rest):
    return lax.optimization_barrier((first, rest))[0] if rest else first


class Line:
    def __init__(self):
        self.waits = ()

    def run(self, kernel, left, *rest, **how):
        if isinstance(left, tuple):
            left = (hold(left[0], *self.waits),) + left[1:]
        else:
            left = hold(left, *self.waits)
        out = kernel(left, *rest, **how)
        self.waits = (out,)
        return out

    def need(self, *arrays):
        self.waits += arrays


class Gather:
    def __init__(self, shards):
        self.shards = shards
        self.columns, self.sides, self.wholes = [], [], []
        self.over = ()
        self.mine = None
        if lax.axis_size("dp") != DIRECT:
            for shard in shards:
                whole = lax.all_gather(shard, "dp", axis=0, tiled=True)
                self.wholes.append((whole, swap_core(whole)))


    def turn(self, *needs):
        if lax.axis_size("dp") != DIRECT:
            return
        me = lax.axis_index("dp")
        first = lax.axis_index("section") == 0
        at = len(self.columns)
        over = self.over + needs
        sent = {}
        if at < len(self.shards):
            rows, width = self.shards[at].shape
            shard = hold(self.shards[at], *over)
            found = swap_dp(shard, 4)
            two = interleave(shard[None], found[None], (me // 4) % 2).reshape(2 * rows, width)
            sent["z"] = swap_dp(two, 8)
        if 0 <= at - 1 < len(self.shards):
            column = hold(self.columns[at - 1], *over)
            sent["xy"] = (swap_dp(column, 1), swap_dp(column, 2))
        if 0 <= at - 2 < len(self.shards):
            from_x, from_y = self.sides[at - 1]
            carried = hold(jnp.where(first, from_x, from_y), *over)
            sent["both"] = swap_split(carried, 2, 1)
        if self.mine is not None:
            sent["core"] = swap_core(hold(self.mine, *over))
        sent = lax.optimization_barrier(sent)
        if "core" in sent:
            self.wholes.append((self.mine, sent["core"]))
        self.mine = None
        new_column = None
        if "z" in sent:
            new_column = interleave(two[None], sent["z"][None], me // 8).reshape(4, rows, width)
        if "both" in sent:
            whole = place_four((self.columns[at - 2], from_x, from_y, sent["both"]))
            self.mine = whole.reshape(-1, whole.shape[-1])
        self.columns.append(new_column)
        self.sides.append(sent.get("xy"))
        self.over = tuple(jax.tree.leaves(sent))


class Sums:
    def __init__(self):
        self.over = ()
        self.sent = {}
        self.kept = (None,) * 4
        self.corner = None
        self.column = None
        self.pair = None
        self.totals = []

    def close(self, summed=None):
        sent, summed = lax.optimization_barrier((self.sent, summed))
        take, take_last, keep, keep_near = self.kept
        self.corner = (take, sent["corner"]) if "corner" in sent else None
        self.column = (take_last,) + sent["xy"] if "xy" in sent else None
        self.pair = keep + sent["far"] if "far" in sent else None
        if "near" in sent:
            self.totals.append(keep_near + sent["near"])
        self.over = tuple(jax.tree.leaves(sent))
        self.sent = {}
        return summed

    def turn(self, summed=None):
        if lax.axis_size("dp") != DIRECT:
            if summed is not None:
                self.totals.append(
                    lax.psum_scatter(summed, "dp", scatter_dimension=0, tiled=True)
                )
            return ()
        me = lax.axis_index("dp")
        y, x = (me // 2) % 2, me % 2
        first = lax.axis_index("section") == 0
        summed = self.close(summed)
        sent, operands = {}, ()

        def split(part, bit):
            keep = lax.dynamic_index_in_dim(part, bit, 0, keepdims=False)
            return keep, lax.dynamic_index_in_dim(part, 1 - bit, 0, keepdims=False)

        if summed is not None:
            rows, width = summed.shape[0] // DIRECT, summed.shape[1]
            blocks = summed.reshape(4, 2, 2, rows, width)

            def take(a, b):
                part = lax.dynamic_slice(blocks, (0, a, b, 0, 0), (4, 1, 1, rows, width))
                return part[:, 0, 0]

            give = hold(take(1 - y, 1 - x), *self.over)
            sent["corner"] = swap_split(give, 1, 2)
            operands += (give,)
        if self.corner is not None:
            take_last, found = self.corner
            to_x = take_last(y, 1 - x) + jnp.where(first, 0.0, found)
            to_y = take_last(1 - y, x) + jnp.where(first, found, 0.0)
            to_x, to_y = hold((to_x, to_y), *self.over)
            sent["xy"] = (swap_dp(to_x, 1), swap_dp(to_y, 2))
            operands += (to_x, to_y)
        if self.column is not None:
            take_old, from_x, from_y = self.column
            part = take_old(y, x) + from_x + from_y
            part = part.reshape((2, 2) + part.shape[1:])
            keep, give = split(part, me // 8)
            give = hold(give, *self.over)
            operands += (give,)
            sent["far"] = swap_dp(give, 8)
        if self.pair is not None:
            keep_near, give = split(self.pair, (me // 4) % 2)
            give = hold(give, *self.over)
            operands += (give,)
            sent["near"] = swap_dp(give, 4)
        self.sent = sent
        self.kept = (
            take if "corner" in sent else None,
            take_last if "xy" in sent else None,
            keep if "far" in sent else None,
            keep_near if "near" in sent else None,
        )
        return self.over + operands


def total_dp(values):
    mask = 1
    while mask < lax.axis_size("dp"):
        values = values + swap_dp(values, mask)
        mask *= 2
    return values


TILE = 256


def parts_of(value):
    high = value.astype(jnp.bfloat16)
    return high, (value - high.astype(jnp.float32)).astype(jnp.bfloat16)


def product(left, right, dims):
    total = None
    for a, b in ((left[0], right[1]), (left[1], right[0]), (left[0], right[0])):
        one = lax.dot_general(a, b, (dims, ((), ())), preferred_element_type=jnp.float32)
        total = one if total is None else total + one
    return total


PLAIN = ((1,), (0,))
FLIPPED = ((1,), (1,))
GRADS = ((0,), (0,))


def kernel_call(body, grid, in_specs, out_shape, out_spec, scratch, depth, prefetch=1):
    return pl.pallas_call(
        body,
        out_shape=jax.ShapeDtypeStruct(out_shape, jnp.float32),
        grid_spec=pltpu.PrefetchScalarGridSpec(
            num_scalar_prefetch=prefetch,
            grid=grid,
            in_specs=in_specs,
            out_specs=out_spec,
            scratch_shapes=scratch,
        ),
        compiler_params=pltpu.CompilerParams(vmem_limit_bytes=52 * 2**20),
        cost_estimate=pl.CostEstimate(
            flops=depth * math.prod(out_shape) // 4, bytes_accessed=0, transcendentals=0
        ),
    )


def section_index():
    return lax.axis_index("section").astype(jnp.int32)[None]


def wide_body(where, left, own, other, *rest, dims, scaled):
    scale = rest[0] if scaled else None
    out, high, low = rest[-3:]

    @pl.when((pl.program_id(0) == 0) & (pl.program_id(1) == 0))
    def _():
        high[...], low[...] = parts_of(left[...])

    def one(right):
        found = product((high[...], low[...]), parts_of(right[...]), dims)
        out[...] = found * scale[...] if scaled else found

    pl.when(pl.program_id(0) == 0)(lambda: one(own))
    pl.when(pl.program_id(0) == 1)(lambda: one(other))


def wide(left, own, other, flipped=False, by_section=False, scale=None, window=None):
    rows, depth = left.shape
    start, columns = window or (0, own.shape[1])
    width = own.shape[0] if flipped else columns
    tile = math.gcd(TILE, width)
    tiles = width // tile
    at = start // columns if flipped else start // tile

    def right(half):
        def index(h, j, where):
            stay = tiles - 1 if half == 0 else 0
            k = jnp.where(h == half, j, stay)
            return (k, at) if flipped else (0, at + k)

        return pl.BlockSpec((tile, depth) if flipped else (depth, tile), index)

    def out_index(h, j, where):
        half = h + where[0] - 2 * h * where[0] if by_section else h
        return (0, half * tiles + j)

    out_spec = pl.BlockSpec((rows, tile), out_index)
    in_specs = [pl.BlockSpec((rows, depth), lambda h, j, where: (0, 0)), right(0), right(1)]
    call = kernel_call(
        partial(wide_body, dims=FLIPPED if flipped else PLAIN, scaled=scale is not None),
        (2, tiles),
        in_specs + ([] if scale is None else [out_spec]),
        (rows, 2 * width),
        out_spec,
        [pltpu.VMEM((rows, depth), jnp.bfloat16)] * 2,
        depth,
    )
    return call(section_index(), left, own, other, *([] if scale is None else [scale]))


def both_body(where, left_own, left_other, own, other, out, *scratch, dims):
    @pl.when(pl.program_id(0) == 0)
    def _():
        scratch[0][...], scratch[1][...] = parts_of(left_own[...])
        scratch[2][...], scratch[3][...] = parts_of(left_other[...])

    found = product((scratch[0][...], scratch[1][...]), parts_of(own[...]), dims)
    out[...] = found + product((scratch[2][...], scratch[3][...]), parts_of(other[...]), dims)


def both(left, own, other, flipped=False, window=None, by_section=False):
    lefts = left if isinstance(left, tuple) else (left, left)
    split = not isinstance(left, tuple)
    rows, depth = lefts[0].shape
    depth = depth // 2 if split else depth
    start, columns = window or (0, own.shape[1])
    width = own.shape[0] if flipped else columns
    tile = math.gcd(TILE, width)
    at = start // columns if flipped else start // tile

    def left_spec(half):
        def index(j, where):
            if not split:
                return (0, 0)
            return (0, (where[0] if half == 0 else 1 - where[0]) if by_section else half)

        return pl.BlockSpec((rows, depth), index)

    def right_index(j, where):
        return (j, at) if flipped else (0, at + j)

    right = pl.BlockSpec((tile, depth) if flipped else (depth, tile), right_index)
    call = kernel_call(
        partial(both_body, dims=FLIPPED if flipped else PLAIN),
        (width // tile,),
        [left_spec(0), left_spec(1), right, right],
        (rows, width),
        pl.BlockSpec((rows, tile), lambda j, where: (0, j)),
        [pltpu.VMEM((rows, depth), jnp.bfloat16)] * 4,
        2 * depth,
    )
    return call(section_index(), lefts[0], lefts[1], own, other)


def grads_body(where, left, right, *rest, added):
    more = rest[0] if added else None
    out, high, low = rest[-3:]

    @pl.when(pl.program_id(0) == 0)
    def _():
        high[...], low[...] = parts_of(right[...])

    found = product(parts_of(left[...]), (high[...], low[...]), GRADS)
    out[...] = found + more[...] if added else found


def grads(left, right, left_half=None, right_half=None, by_section=False, more=None):
    rows = left.shape[0]
    depth = left.shape[1] if left_half is None else left.shape[1] // 2
    width = right.shape[1] if right_half is None else right.shape[1] // 2
    tile = math.gcd(TILE, depth)
    tiles = depth // tile
    first = 0 if left_half is None else left_half * tiles

    def right_index(k, where):
        if right_half is None:
            return (0, 0)
        if by_section:
            return (0, where[0] if right_half == 0 else 1 - where[0])
        return (0, right_half)

    out_spec = pl.BlockSpec((tile, width), lambda k, where: (k, 0))
    in_specs = [
        pl.BlockSpec((rows, tile), lambda k, where: (0, first + k)),
        pl.BlockSpec((rows, width), right_index),
    ]
    call = kernel_call(
        partial(grads_body, added=more is not None),
        (tiles,),
        in_specs + ([] if more is None else [out_spec]),
        (depth, width),
        out_spec,
        [pltpu.VMEM((rows, width), jnp.bfloat16)] * 2,
        rows,
    )
    return call(section_index(), left, right, *([] if more is None else [more]))


def grads_pair_body(where, left, right, left_out, right_out, *rest, added):
    more = rest[0] if added else None
    out, high, low, high_out, low_out = rest[-5:]

    @pl.when(pl.program_id(0) == 0)
    def _():
        high[...], low[...] = parts_of(right[...])
        high_out[...], low_out[...] = parts_of(right_out[...])

    cut = right.shape[1]
    found = product(parts_of(left[...]), (high[...], low[...]), GRADS)
    out[:, :cut] = found + more[:, :cut] if added else found
    found = product(parts_of(left_out[...]), (high_out[...], low_out[...]), GRADS)
    out[:, cut:] = found + more[:, cut:] if added else found


def grads_pair(left, right, left_out, right_out, half, more=None):
    rows, depth = left.shape
    width, width_out = right.shape[1] // 2, right_out.shape[1] // 2
    tile = math.gcd(TILE, depth)
    out_spec = pl.BlockSpec((tile, width + width_out), lambda k, where: (k, 0))
    left_spec = pl.BlockSpec((rows, tile), lambda k, where: (0, k))

    def by_section(k, where):
        return (0, where[0] if half == 0 else 1 - where[0])

    in_specs = [
        left_spec,
        pl.BlockSpec((rows, width), lambda k, where: (0, half)),
        left_spec,
        pl.BlockSpec((rows, width_out), by_section),
    ]
    call = kernel_call(
        partial(grads_pair_body, added=more is not None),
        (depth // tile,),
        in_specs + ([] if more is None else [out_spec]),
        (depth, width + width_out),
        out_spec,
        [pltpu.VMEM((rows, width), jnp.bfloat16)] * 2
        + [pltpu.VMEM((rows, width_out), jnp.bfloat16)] * 2,
        rows,
    )
    return call(
        section_index(), left, right, left_out, right_out, *([] if more is None else [more])
    )


def weigh(where, slopes, query, keys, head):
    rows, lanes = query.shape
    scores = product(parts_of(query), keys, FLIPPED) * (lanes // 2) ** (-0.5)
    queries = lax.broadcasted_iota(jnp.int32, (rows, rows), 0)
    positions = lax.broadcasted_iota(jnp.int32, (rows, rows), 1)
    distance = jnp.abs(queries - positions).astype(jnp.float32)
    scores = scores - slopes[head] * distance
    scores = jnp.where(positions < where[1], scores, MASKED)
    weighted = jnp.exp(scores - jnp.max(scores, axis=-1, keepdims=True))
    return weighted, 1.0 / jnp.sum(weighted, axis=-1, keepdims=True)


def of_head(block, which):
    lanes = lax.broadcasted_iota(jnp.int32, block.shape, 1)
    half = block.shape[1] // 2
    mine = lanes < half if which == 0 else lanes >= half
    return jnp.where(mine, block, 0.0), mine


def attend_body(where, slopes, projected, out):
    lanes = out.shape[1]
    query, key, value = [projected[:, k * lanes : (k + 1) * lanes] for k in range(3)]
    keys, values = parts_of(key), parts_of(value)
    found = []
    for which in range(2):
        mine_query, mine = of_head(query, which)
        weighted, scale = weigh(where, slopes, mine_query, keys, 2 * pl.program_id(0) + which)
        found.append(product(parts_of(weighted), values, PLAIN) * scale)
    out[...] = jnp.where(mine, found[1], found[0])


def attend_back_body(where, slopes, projected, grad, out):
    lanes = grad.shape[1]
    query, key, value = [projected[:, k * lanes : (k + 1) * lanes] for k in range(3)]
    queries, keys, values = parts_of(query), parts_of(key), parts_of(value)
    grad_parts = parts_of(grad[...])
    found = []
    for which in range(2):
        mine_query, mine = of_head(query, which)
        weighted, scale = weigh(where, slopes, mine_query, keys, 2 * pl.program_id(0) + which)
        probability = weighted * scale
        mine_grad, _ = of_head(grad[...], which)
        back = product(parts_of(mine_grad), values, FLIPPED)
        back = probability * (back - jnp.sum(probability * back, axis=-1, keepdims=True))
        back = parts_of(back * (lanes // 2) ** (-0.5))
        found.append(
            (
                product(back, keys, PLAIN),
                product(back, queries, GRADS),
                product(parts_of(probability), grad_parts, GRADS),
            )
        )
    for k in range(3):
        out[:, k * lanes : (k + 1) * lanes] = jnp.where(mine, found[1][k], found[0][k])


def head_pairs(body, projected, length, grad=None):
    rows = projected.shape[0]
    pairs = HEADS // 2
    half = pairs // 2
    lanes = projected.shape[1] // (3 * pairs)
    section = lax.axis_index("section")
    ids = jnp.stack([section, 1 - section])[:, None] * (HEADS // 2) + jnp.arange(HEADS // 2)
    slopes = 2.0 ** (-8.0 * (ids.reshape(-1).astype(jnp.float32) + 1.0) / HEADS)

    def in_place(p, where, slopes):
        own = p // half
        return (0, (own + where[0] - 2 * own * where[0]) * half + p % half)

    wide_spec = pl.BlockSpec((rows, 3 * lanes), lambda p, where, slopes: (0, p))
    one_spec = pl.BlockSpec((rows, lanes), in_place)
    call = kernel_call(
        body,
        (pairs,),
        [wide_spec] if grad is None else [wide_spec, one_spec],
        (rows, lanes * pairs) if grad is None else projected.shape,
        one_spec if grad is None else wide_spec,
        [],
        rows,
        prefetch=2,
    )
    where = jnp.stack([section.astype(jnp.int32), length.astype(jnp.int32)])
    return call(where, slopes, projected, *([] if grad is None else [grad]))


def attend(projected, length):
    return head_pairs(attend_body, projected, length)


def attend_back(projected, grad, length):
    return head_pairs(attend_back_body, projected, length, grad)


def interleave_body(where, mine, given, out):
    @pl.when(pl.program_id(1) == 0)
    def _():
        out[0, 0] = mine[0]

    @pl.when(pl.program_id(1) == 1)
    def _():
        out[0, 0] = given[0]


def interleave(mine, given, bit):
    count, rows, width = mine.shape
    block = pl.BlockSpec((1, rows, width), lambda a, k, where: (a, 0, 0))
    out_spec = pl.BlockSpec(
        (1, 1, rows, width), lambda a, k, where: (a, where[0] + k - 2 * k * where[0], 0, 0)
    )
    call = kernel_call(
        interleave_body, (count, 2), [block, block], (count, 2, rows, width), out_spec, [], 0
    )
    return call(bit.astype(jnp.int32)[None], mine, given)


def place_body(where, own, from_x, from_y, from_both, out):
    for k, part in enumerate((own, from_x, from_y, from_both)):

        @pl.when(pl.program_id(0) == k)
        def _():
            out[0, 0, 0] = part[0]


def place_four(parts):
    count, rows, width = parts[0].shape
    me = lax.axis_index("dp")

    def part_spec(which):
        def index(k, a, where):
            return (jnp.where(k == which, a, jnp.where(k < which, 0, count - 1)), 0, 0)

        return pl.BlockSpec((1, rows, width), index)

    def out_index(k, a, where):
        y, x = k // 2, k % 2
        return (a, where[0] + y - 2 * y * where[0], where[1] + x - 2 * x * where[1], 0, 0)

    call = kernel_call(
        place_body,
        (4, count),
        [part_spec(which) for which in range(4)],
        (count, 2, 2, rows, width),
        pl.BlockSpec((1, 1, 1, rows, width), out_index),
        [],
        0,
    )
    return call(jnp.stack([(me // 2) % 2, me % 2]).astype(jnp.int32), *parts)


def normalise(stream):
    centered = stream - jnp.mean(stream, axis=-1, keepdims=True)
    spread = jnp.mean(centered * centered, axis=-1, keepdims=True)
    inverse = lax.rsqrt(spread + EPS)
    return (centered * inverse, inverse)


def norm_backward(grad, unit, inverse, gain):
    scaled = grad * gain
    back = scaled - jnp.mean(scaled, axis=-1, keepdims=True)
    back = back - unit * jnp.mean(scaled * unit, axis=-1, keepdims=True)
    return (inverse * back, jnp.sum(grad * unit, axis=0), jnp.sum(grad, axis=0))


def windows(stream):
    half = stream.shape[1] // 2
    return (0, 3 * half), (3 * half, half)


def attention_forward(stream, gain, shift, weights, length, line):
    window_in, window_out = windows(stream)
    unit, inverse = normalise(stream)
    normed = unit * gain + shift
    projected = line.run(wide, normed, *weights, window=window_in)
    context = line.run(attend, projected, length)
    out = stream + line.run(wide, context, *weights, window=window_out, by_section=True)
    return (out, (unit, inverse, gain, normed, projected, context))


def attention_backward(grad, saved, weights, length, line, send, under_way):
    unit, inverse, gain, normed, projected, context = saved
    window_in, window_out = windows(grad)
    back = line.run(both, grad, *weights, flipped=True, window=window_out, by_section=True)
    back = line.run(lambda g: attend_back(projected, g, length), back)
    line.need(*under_way())
    given = swap_core(line.run(grads_pair, normed, back, context, grad, 1))
    normed_grad = line.run(both, back, *weights, flipped=True, window=window_in)
    send(line.run(grads_pair, normed, back, context, grad, 0, more=given))
    stream_grad, gain_grad, shift_grad = norm_backward(normed_grad, unit, inverse, gain)
    return (grad + stream_grad, gain_grad, shift_grad)


def feed_forward(stream, gain, shift, weights, line):
    up_own, up_other, down_own, down_other = weights
    unit, inverse = normalise(stream)
    normed = unit * gain + shift
    inner = line.run(wide, normed, up_own, up_other)
    bell = jnp.exp(-0.5 * inner * inner) * 0.3989422804014327
    below = 0.5 * (1.0 + lax.erf(inner * 0.7071067811865476))
    hidden = inner * below
    slope = below + inner * bell

    def finish():
        return stream + line.run(both, hidden, down_own, down_other)

    return (finish, (unit, inverse, gain, normed, hidden, slope))


def feed_backward(grad, saved, weights, line, between, send_down, send_up):
    up_own, up_other, down_own, down_other = weights
    unit, inverse, gain, normed, hidden, slope = saved
    down_given = swap_core(line.run(grads, hidden, grad, left_half=1))
    between(0)
    back = line.run(wide, grad, down_own, down_other, flipped=True, scale=slope)
    up_given = swap_core(line.run(grads, normed, back, right_half=1))
    between(1)
    send_down(line.run(grads, hidden, grad, left_half=0, more=down_given))
    normed_grad = line.run(both, back, up_own, up_other, flipped=True)
    send_up(line.run(grads, normed, back, right_half=0, more=up_given))
    stream_grad, gain_grad, shift_grad = norm_backward(normed_grad, unit, inverse, gain)
    return (grad + stream_grad, gain_grad, shift_grad)


def local_moments(grad, rows_old, weight):
    squared = grad * grad + TINY
    rows_new = DECAY * rows_old + (1.0 - DECAY) * jnp.mean(squared, axis=1)
    scaled = jnp.sum(grad * grad / rows_new[:, None], axis=0)
    pair = jnp.stack([jnp.sum(rows_new), jnp.sum(weight * weight)])
    return (rows_new, [jnp.sum(squared, axis=0), scaled, pair])


def finish(grad, weight, rows_new, cols_old, totals, total_rows):
    column_total, scaled_total, pair = totals
    cols_new = DECAY * cols_old + (1.0 - DECAY) * (column_total / total_rows)
    rows_mean = pair[0] / total_rows
    second = rows_new[:, None] * cols_new[None, :] / rows_mean
    update = grad * lax.rsqrt(second)
    count = total_rows * grad.shape[1]
    ratio = jnp.sqrt(rows_mean * jnp.sum(scaled_total / cols_new) / count) / CLIP
    scale = jnp.maximum(jnp.sqrt(pair[1] / count), FLOOR)
    return (cols_new, weight - RHO * scale * (update / jnp.maximum(ratio, 1.0)))


def on_device(
    frames,
    cotangent,
    lengths,
    attn_in,
    attn_out,
    ffn_up,
    ffn_down,
    norm_params,
    skip_proj,
    in_rows,
    in_cols,
    out_rows,
    out_cols,
    up_rows,
    up_cols,
    down_rows,
    down_cols,
    skip_rows,
    skip_cols,
    norm_moment,
):
    section = lax.axis_index("section")
    me = lax.axis_index("dp")
    data_size = lax.axis_size("dp")
    first = section == 0
    frame_count, model_width = frames.shape[2], frames.shape[3]
    width = model_width // 2
    share = attn_in.shape[1]
    hidden_block = ffn_down.shape[1] // 2
    lanes = 2 * model_width // HEADS
    source = lax.dynamic_index_in_dim(frames, section, 0, keepdims=False)[0]
    length = lax.dynamic_index_in_dim(lengths, section, 0, keepdims=False)[0]
    valid_rows = (jnp.arange(frame_count) < length).astype(jnp.float32)[:, None]
    outer = lax.dynamic_index_in_dim(cotangent, section, 0, keepdims=False)[0] * valid_rows

    def attn_half(s):
        split = attn_in[0].reshape(share, 3, 2, -1, lanes)
        inner = lax.dynamic_index_in_dim(split, s, 2, keepdims=False).swapaxes(1, 2)
        outward = lax.dynamic_slice_in_dim(attn_out[0], s * width, width, 1)
        return jnp.concatenate([inner.reshape(share, 3 * width), outward], 1)

    def up_half(shard, s):
        split = shard[0].reshape(share, data_size, 2, hidden_block)
        return lax.dynamic_index_in_dim(split, s, 2, keepdims=False).reshape(share, -1)

    def down_half(shard, s):
        return lax.dynamic_slice_in_dim(shard[0], s * hidden_block, hidden_block, 0)

    def by_owner(half):
        kept = half(section)
        given = swap_core(half(1 - section))
        return (jnp.where(first, kept, given), jnp.where(first, given, kept))

    norm_shard = jnp.pad(norm_params[0].T, ((0, 0), (0, PAD - norm_params.shape[1])))
    attn_zero, attn_one = by_owner(attn_half)
    attn_zero = jnp.concatenate([attn_zero, norm_shard], 1)
    (ffn_up_held, ffn_down_held), _ = lax.optimization_barrier(((ffn_up, ffn_down), attn_zero))
    up_zero, up_one = by_owner(partial(up_half, ffn_up_held))
    down_zero, down_one = by_owner(partial(down_half, ffn_down_held))
    gather = Gather([attn_zero, down_one, skip_proj, attn_one])

    def gather_beside(shard, *needs):
        whole = lax.all_gather(shard, "dp", axis=0, tiled=True)
        return (whole, swap_core(hold(whole, *needs)))

    line = Line()
    for _ in range(5):
        gather.turn()
    attn_zero_full = gather.wholes[0]
    norms = [full[:, 4 * width : 4 * width + 4].T for full in attn_zero_full]
    norm_zero = jnp.where(first, norms[0], norms[1])
    norm_one = jnp.where(first, norms[1], norms[0])
    after_attn, saved_a0 = attention_forward(
        source, norm_zero[0], norm_zero[1], attn_zero_full, length, line
    )
    gather.turn(after_attn)
    ffn_one_full = gather_beside(up_one) + gather.wholes[1]
    finish_twelve, saved_f1 = feed_forward(
        after_attn, norm_one[2], norm_one[3], ffn_one_full, line
    )
    twelve = finish_twelve()
    gather.turn(twelve)
    skip_full, attn_one_full = gather.wholes[2:]
    joined_own = jnp.where(first, twelve, source)
    joined_other = jnp.where(first, source, twelve)
    joined = line.run(both, (joined_own, joined_other), *skip_full)
    middle, saved_a1 = attention_forward(
        joined, norm_one[0], norm_one[1], attn_one_full, length, line
    )
    ffn_zero_full = gather_beside(up_zero) + gather_beside(down_zero, joined)
    finish_thirteen, saved_f0 = feed_forward(
        middle, norm_zero[2], norm_zero[3], ffn_zero_full, line
    )

    sums = Sums()
    late = []

    def send(summed):
        line.need(*sums.turn(summed))

    def under_way():
        return sums.sent.get("xy", ()) + ((sums.sent["far"],) if "far" in sums.sent else ())

    def between(step):
        return None

    grad, g02, g03 = feed_backward(
        outer, saved_f0, ffn_zero_full, line, between, send, send
    )
    thirteen = finish_thirteen()
    grad, g10, g11 = attention_backward(grad, saved_a1, attn_one_full, length, line, send, under_way)
    skip_given = swap_core(line.run(grads, joined_other, grad))
    back = line.run(wide, grad, *skip_full, flipped=True, by_section=True)
    joined_grad = grad
    grad, frames_grad = back[:, :model_width], back[:, model_width:]

    def between(step):
        if step == 0:
            late.append(line.run(grads, joined_own, joined_grad, more=skip_given))
            line.need(*under_way())
        else:
            send(late[0])

    grad, g12, g13 = feed_backward(grad, saved_f1, ffn_one_full, line, between, send, send)
    after_attn_grad = grad
    grad, g00, g01 = attention_backward(grad, saved_a0, attn_zero_full, length, line, send, under_way)
    frames_grad = frames_grad + grad
    norm_grads = total_dp(jnp.stack([g00, g01, g02, g03, g10, g11, g12, g13]))
    norm_grads = (norm_grads + swap_core(norm_grads)).reshape(2, 4, model_width)
    norm_share = lax.dynamic_slice(norm_grads, (section, 0, me * share), (1, 4, share))[0]
    for _ in range(3):
        sums.turn()
    sums.close()
    down_zero_s, up_zero_s, attn_one_s, skip_grad, down_one_s, up_one_s, attn_zero_s = sums.totals

    def to_owner(zero, one):
        kept = jnp.where(first, zero, one)
        given = swap_core(jnp.where(first, one, zero))
        return (jnp.where(first, kept, given), jnp.where(first, given, kept))

    def in_columns(part):
        split = part[:, : 3 * width].reshape(share, -1, 3, lanes).swapaxes(1, 2)
        return split.reshape(share, 3, width)

    attn_pair = to_owner(attn_zero_s, attn_one_s)
    up_pair = to_owner(up_zero_s, up_one_s)
    shares = [
        jnp.stack([in_columns(part) for part in attn_pair], 2).reshape(share, -1),
        jnp.concatenate([part[:, 3 * width :] for part in attn_pair], 1),
        jnp.stack([part.reshape(share, data_size, -1) for part in up_pair], 2).reshape(share, -1),
        jnp.concatenate(to_owner(down_zero_s, down_one_s), 0),
    ]

    current = [attn_in[0], attn_out[0], ffn_up[0], ffn_down[0]]
    rows_old = [in_rows[0], out_rows[0], up_rows[0], down_rows[0]]
    cols_old = [in_cols[0], out_cols[0], up_cols[0], down_cols[0]]
    moments = [local_moments(g, r, w) for g, r, w in zip(shares, rows_old, current)]
    skip_rows_new, skip_local = local_moments(skip_grad, skip_rows, skip_proj)
    norm_moment_new = DECAY * norm_moment[0] + (1.0 - DECAY) * (norm_share * norm_share + TINY)
    norm_raw = norm_share * lax.rsqrt(norm_moment_new)
    norm_sums = [
        jnp.sum(norm_raw * norm_raw, axis=-1),
        jnp.sum(norm_params[0] * norm_params[0], axis=-1),
    ]
    vectors = skip_local + [v for _, local in moments for v in local] + norm_sums
    sizes = [v.shape[0] for v in vectors]
    packed = jnp.concatenate(vectors)
    packed = total_dp(jnp.pad(packed, (0, -packed.shape[0] % PAD)))
    skip_size = sum(sizes[:3])
    skip_totals = packed[:skip_size] + swap_core(packed[:skip_size])
    offsets = [sum(sizes[:k]) for k in range(len(sizes))]
    totals = [packed[at : at + size] for at, size in zip(offsets, sizes)]
    updated = [
        finish(
            shares[k],
            current[k],
            moments[k][0],
            cols_old[k],
            totals[3 + 3 * k : 6 + 3 * k],
            shares[k].shape[0] * data_size,
        )
        for k in range(4)
    ]
    skip_cols_new, skip_new = finish(
        skip_grad,
        skip_proj,
        skip_rows_new,
        skip_cols,
        [skip_totals[at : at + size] for at, size in zip(offsets[:3], sizes[:3])],
        skip_grad.shape[0] * data_size * 2,
    )
    norm_ratio = jnp.sqrt(totals[15] / model_width) / CLIP
    norm_scale = jnp.maximum(jnp.sqrt(totals[16] / model_width), FLOOR)
    norms_new = norm_params[0] - RHO * norm_scale[:, None] * (
        norm_raw / jnp.maximum(norm_ratio, 1.0)[:, None]
    )

    def both_micro(zero, one):
        kept = jnp.where(first, zero, one)
        given = swap_core(jnp.where(first, one, zero))
        pair = jnp.where(first, jnp.stack([kept, given]), jnp.stack([given, kept]))
        return pair[None, :, None]

    layer_outputs = both_micro(thirteen, twelve)
    input_grads = both_micro(frames_grad, after_attn_grad)
    return (
        layer_outputs,
        input_grads,
        shares[0][None],
        moments[0][0][None],
        updated[0][0][None],
        updated[0][1][None],
        shares[1][None],
        moments[1][0][None],
        updated[1][0][None],
        updated[1][1][None],
        shares[2][None],
        moments[2][0][None],
        updated[2][0][None],
        updated[2][1][None],
        shares[3][None],
        moments[3][0][None],
        updated[3][0][None],
        updated[3][1][None],
        skip_grad,
        skip_rows_new,
        skip_cols_new,
        skip_new,
        norm_share[None],
        norm_moment_new[None],
        norms_new[None],
    )


def solution(mesh):
    return jax.shard_map(
        on_device,
        mesh=mesh,
        in_specs=(
            P(None, "dp", None, None),
            P(None, "dp", None, None),
            P(None, "dp"),
            P("section", "dp", None),
            P("section", "dp", None),
            P("section", "dp", None),
            P("section", "dp", None),
            P("section", None, "dp"),
            P(("section", "dp"), None),
            P("section", "dp"),
            P("section", None),
            P("section", "dp"),
            P("section", None),
            P("section", "dp"),
            P("section", None),
            P("section", "dp"),
            P("section", None),
            P(("section", "dp")),
            P(),
            P("section", None, "dp"),
        ),
        out_specs=(
            P("section", None, "dp", None, None),
            P("section", None, "dp", None, None),
            P("section", "dp", None),
            P("section", "dp"),
            P("section", None),
            P("section", "dp", None),
            P("section", "dp", None),
            P("section", "dp"),
            P("section", None),
            P("section", "dp", None),
            P("section", "dp", None),
            P("section", "dp"),
            P("section", None),
            P("section", "dp", None),
            P("section", "dp", None),
            P("section", "dp"),
            P("section", None),
            P("section", "dp", None),
            P(("section", "dp"), None),
            P(("section", "dp")),
            P(),
            P(("section", "dp"), None),
            P("section", None, "dp"),
            P("section", None, "dp"),
            P("section", None, "dp"),
        ),
        check_vma=False,
    )
```

time: 1580 us -> 1510 us (0.956)
  Pallas kernels: 0 us -> 457 us
  matrix products: 374 us -> 0 us
  starting transfers between devices: 308 us -> 74.1 us
  waiting for transfers between devices: 534 us -> 704 us
  local copies, waits for them, and re-layouts: 214 us -> 87 us
  other arithmetic: 128 us -> 152 us
    pallas_call x0 -> x48, Pallas kernels: none -> 457 us  [the longest x9 120 us: wide(): call(section_index(), left, own, other, *([] if scale is None else [scale]))]
    dot_general x78 -> x0, matrix products: 374 us -> none  [the longest x18 119 us: dot(): return jnp.dot(left, right, precision=PRECISE)]
    ppermute x88 -> x52, waiting for transfers between devices: 420 us -> 633 us  [swap_dp(): lax.ppermute(block, 'dp', [(i, i ^ mask) for i in range(lax.axis_size('dp...]
    ppermute x88 -> x52, starting transfers between devices: 208 us -> 31.2 us  [swap_dp(): lax.ppermute(block, 'dp', [(i, i ^ mask) for i in range(lax.axis_size('dp...]
    dynamic_update_slice x62 -> x0, local copies, waits for them, and re-layouts: 81.5 us -> none  [the longest x10 18.6 us: assemble(): lax.dynamic_update_slice(whole, from_both[:, None, None], (0, 1 - y, 1 -...]
    ppermute x30 -> x24, starting transfers between devices: 87 us -> 31.1 us  [swap_core(): return lax.ppermute(block, 'section', [(0, 1), (1, 0)])]
    ppermute x16 -> x11, waiting for transfers between devices: 113 us -> 67 us  [swap_split(): return lax.ppermute(block, ('section', 'dp'), route)]
    add x23 -> x29, other arithmetic: 43.4 us -> 75.3 us  [the longest x7 35.4 us: turn(): to_y = take_last(1 - y, x) + jnp.where(first, found, 0.0)]
  transfers between devices with their start and end apart: 134 -> 90, of which waited for: 55 -> 42; matrix products, arithmetic and copies ran while one was open for 42% -> 12% of each run, Pallas kernels for 0% -> 29%
where the time goes in v2:
time: 1510 us; the launch traced here: 1500 us
  waiting for transfers between devices  704 us (47%)
  Pallas kernels  457 us (30%)
  other arithmetic  152 us (10%)
  local copies, waits for them, and re-layouts  87 us (6%)
  starting transfers between devices  74.1 us (5%)
  between operations  26.1 us (2%)
    ppermute x52, waiting for transfers between devices, swap_dp(): lax.ppermute(block, 'dp', [(i, i ^ mask) for i in range(lax.axis_size('dp...  633 us
    pallas_call x9, Pallas kernels, wide(): call(section_index(), left, own, other, *([] if scale is None else [scale]))  120 us
    pallas_call x10, Pallas kernels, grads(): return call(section_index(), left, right, *([] if more is None else [more]))  88.8 us
    pallas_call x9, Pallas kernels, both(): return call(section_index(), lefts[0], lefts[1], own, other)  84.7 us
    ppermute x11, waiting for transfers between devices, swap_split(): return lax.ppermute(block, ('section', 'dp'), route)  67 us
    pallas_call x4, Pallas kernels, head_pairs(): return call(where, slopes, projected, *([] if grad is None else [grad]))  60.7 us
    pallas_call x4, Pallas kernels, place_four(): return call(jnp.stack([me // 2 % 2, me % 2]).astype(jnp.int32), *parts)  53.1 us
    pallas_call x4, Pallas kernels, grads_pair(): call(section_index(), left, right, left_out, right_out, *([] if more is N...  37.4 us
  transfers between devices with their start and end apart: 90, of which 42 were waited for; matrix products, arithmetic and copies ran while one was open for 12% of the time, Pallas kernels for 29%

profile of v2, /device:TPU:1, one launch (start us, length us, event | category | flops | bytes accessed | tf_op | source)
XLA Modules:
  0.0 1500.6 jit_solution(6517778236391845280)
XLA Ops:
  20.7 15.6 %collective-permute-done.1 = f32[64,2176]{1,0:T(8,128)S(1)} collective-permute-done((f32[64,2176]{1,0:T(8,128)S(1)}, f32[64,2176]{1,0:T(8,128)S(1)}, u32[]{:S(2)}, u32[]{:S(2)}) %collective-permute-start.1) | collective-permute-done | bytes 557088 | tf_op jit(solution)/shard_map/ppermute | solution.py:31
  44.0 72.5 %collective-permute-done.2 = f32[128,2176]{1,0:T(8,128)S(1)} collective-permute-done((f32[128,2176]{1,0:T(8,128)}, f32[128,2176]{1,0:T(8,128)S(1)}, u32[]{:S(2)}, u32[]{:S(2)}) %collective-permute-start.2) | collective-permute-done | bytes 1114144 | tf_op jit(solution)/shard_map/ppermute | solution.py:31
  127.0 31.4 %collective-permute-done.6 = f32[128,1024]{1,0:T(8,128)S(1)} collective-permute-done((f32[128,1024]{1,0:T(8,128)S(1)}, f32[128,1024]{1,0:T(8,128)S(1)}, u32[]{:S(2)}, u32[]{:S(2)}) %collective-permute-start.6) | collective-permute-done | bytes 524320 | tf_op jit(solution)/shard_map/ppermute | solution.py:31
  159.4 66.7 %collective-permute-done.7 = f32[256,1024]{1,0:T(8,128)S(1)} collective-permute-done((f32[256,1024]{1,0:T(8,128)}, f32[256,1024]{1,0:T(8,128)S(1)}, u32[]{:S(2)}, u32[]{:S(2)}) %collective-permute-start.7) | collective-permute-done | bytes 1048608 | tf_op jit(solution)/shard_map/ppermute | solution.py:31
  247.6 42.1 %collective-permute-done.12 = f32[128,1024]{1,0:T(8,128)S(1)} collective-permute-done((f32[128,1024]{1,0:T(8,128)S(1)}, f32[128,1024]{1,0:T(8,128)S(1)}, u32[]{:S(2)}, u32[]{:S(2)}) %collective-permute-start.12) | collective-permute-done | bytes 524320 | tf_op jit(solution)/shard_map/ppermute | solution.py:31
  289.8 56.3 %collective-permute-done.9.from_x = f32[4,128,1024]{2,1,0:T(8,128)} collective-permute-done((f32[4,128,1024]{2,1,0:T(8,128)}, f32[4,128,1024]{2,1,0:T(8,128)}, u32[]{:S(2)}, u32[]{:S(2)}) %collective-permute-start.9) | collective-permute-done | bytes 2097184 | tf_op jit(solution)/shard_map/ppermute | solution.py:31
  378.8 31.7 %collective-permute-done.15.from_x = f32[4,64,1024]{2,1,0:T(8,128)S(1)} collective-permute-done((f32[4,64,1024]{2,1,0:T(8,128)}, f32[4,64,1024]{2,1,0:T(8,128)S(1)}, u32[]{:S(2)}, u32[]{:S(2)}) %collective-permute-start.15) | collective-permute-done | bytes 1048608 | tf_op jit(solution)/shard_map/ppermute | solution.py:31
  410.5 16.9 %collective-permute-done.18 = f32[128,2048]{1,0:T(8,128)S(1)} collective-permute-done((f32[128,2048]{1,0:T(8,128)}, f32[128,2048]{1,0:T(8,128)S(1)}, u32[]{:S(2)}, u32[]{:S(2)}) %collective-permute-start.18) | collective-permute-done | bytes 1048608 | tf_op jit(solution)/shard_map/ppermute | solution.py:31
  488.9 37.7 %collective-permute-done.21.from_both = f32[4,64,1024]{2,1,0:T(8,128)S(1)} collective-permute-done((f32[4,64,1024]{2,1,0:T(8,128)S(1)}, f32[4,64,1024]{2,1,0:T(8,128)S(1)}, u32[]{:S(2)}, u32[]{:S(2)}) %collective-permute-start.21) | collective-permute-done | bytes 1048608 | tf_op jit(solution)/shard_map/ppermute | solution.py:38
  543.4 17.9 %shard_map.398 = f32[256,4096]{1,0:T(8,128)} custom-call(s32[1]{0:T(128)} %bitcast.where, f32[256,1024]{1,0:T(8,128)S(1)} %multiply_add_fusion.5.left, f32[1024,2048]{1,0:T(8,128)} %all-gather.4.cloned.1.call-done.own, f32[1024,2048]{1,0:T(8,128)} %collective-permute-done.20.other), custom_call_target="tpu_custom_call" | custom-call | flops 268435456 | tf_op jit(solution)/shard_map/pallas_call | solution.py:290
  582.2 14.6 shard_map.404
  643.2 17.5 %shard_map.408 = f32[256,4096]{1,0:T(8,128)} custom-call(s32[1]{0:T(128)} %bitcast.where, f32[256,1024]{1,0:T(8,128)S(1)} %multiply_add_fusion.3.left, f32[1024,2048]{1,0:T(8,128)} %all-gather.6.cloned.1.call-done.own, f32[1024,2048]{1,0:T(8,128)} %collective-permute-done.28.other), custom_call_target="tpu_custom_call" | custom-call | flops 268435456 | tf_op jit(solution)/shard_map/pallas_call | solution.py:290
  676.3 18.4 %shard_map.410.right.left_own.left_other = f32[256,4096]{1,0:T(8,128)} custom-call(s32[1]{0:T(128)} %bitcast.where, f32[256,1024]{1,0:T(8,128)S(1)} %copy-done.7, f32[2048,1024]{1,0:T(8,128)} %all-gather.8.cloned.1.call-done.own, f32[2048,1024]{1,0:T(8,128)} %collective-permute-done.29.other, f32[256,4096]{1,0:T(8,128)} %get-tuple-element.406.rest_0_), custom_call_target="tpu_custom_call" | custom-call | flops 268435456 | tf_op jit(solution)/shard_map/pallas_call | solution.py:290
  775.4 18.6 %shard_map.417.right.left_own.left_other = f32[256,3072]{1,0:T(8,128)} custom-call(s32[2]{0:T(128)S(1)} %pad_add_fusion.where, f32[16]{0:T(128)S(1)} %reshape.897.slopes, f32[256,3072]{1,0:T(8,128)} %shard_map.405.projected, f32[256,1024]{1,0:T(8,128)S(1)} %shard_map.416.grad), custom_call_target="tpu_custom_call" | custom-call | flops 50331648 | tf_op jit(solution)/shard_map/pallas_call | solution.py:510
  881.2 34.5 %collective-permute-done.41 = f32[2,128,1024]{2,1,0:T(8,128)S(1)} collective-permute-done((f32[2,128,1024]{2,1,0:T(8,128)S(1)}, f32[2,128,1024]{2,1,0:T(8,128)S(1)}, u32[]{:S(2)}, u32[]{:S(2)}) %collective-permute-start.41) | collective-permute-done | bytes 1048608 | tf_op jit(solution)/shard_map/ppermute | solution.py:31
  918.1 19.0 %shard_map.425.right.left_own.left_other = f32[256,4096]{1,0:T(8,128)} custom-call(s32[1]{0:T(128)} %bitcast.where, f32[256,1024]{1,0:T(8,128)S(1)} %slice.182.right.left, f32[2048,1024]{1,0:T(8,128)} %bitcast.395, f32[2048,1024]{1,0:T(8,128)} %collective-permute-done.22.other, f32[256,4096]{1,0:T(8,128)} %get-tuple-element.404.rest_0_), custom_call_target="tpu_custom_call" | custom-call | flops 268435456 | tf_op jit(solution)/shard_map/pallas_call | solution.py:290
  947.5 24.2 %collective-permute-done.42 = f32[4,64,2048]{2,1,0:T(8,128)} collective-permute-done((f32[4,64,2048]{2,1,0:T(8,128)}, f32[4,64,2048]{2,1,0:T(8,128)}, u32[]{:S(2)}, u32[]{:S(2)}) %collective-permute-start.42) | collective-permute-done | bytes 2097184 | tf_op jit(solution)/shard_map/ppermute | solution.py:38
  1005.6 35.8 %collective-permute-done.45 = f32[2,64,2048]{2,1,0:T(8,128)S(1)} collective-permute-done((f32[2,64,2048]{2,1,0:T(8,128)S(1)}, f32[2,64,2048]{2,1,0:T(8,128)S(1)}, u32[]{:S(2)}, u32[]{:S(2)}) %collective-permute-start.45) | collective-permute-done | bytes 1048608 | tf_op jit(solution)/shard_map/ppermute | solution.py:31
  1117.6 18.2 %shard_map.431.right.left_own.left_other = f32[256,3072]{1,0:T(8,128)} custom-call(s32[2]{0:T(128)S(1)} %pad_add_fusion.where, f32[16]{0:T(128)S(1)} %reshape.897.slopes, f32[256,3072]{1,0:T(8,128)} %shard_map.395.projected, f32[256,1024]{1,0:T(8,128)S(1)} %shard_map.430.grad), custom_call_target="tpu_custom_call" | custom-call | flops 50331648 | tf_op jit(solution)/shard_map/pallas_call | solution.py:510
  1204.8 32.7 %collective-permute-done.77 = f32[8,1024]{1,0:T(8,128)S(1)} collective-permute-done((f32[8,1024]{1,0:T(8,128)S(1)}, f32[8,1024]{1,0:T(8,128)S(1)}, u32[]{:S(2)}, u32[]{:S(2)}) %collective-permute-start.77) | collective-permute-done | bytes 32800 | tf_op jit(solution)/shard_map/ppermute | solution.py:31
  1239.4 22.0 %collective-permute-done.78 = f32[8,1024]{1,0:T(8,128)S(1)} collective-permute-done((f32[8,1024]{1,0:T(8,128)S(1)}, f32[8,1024]{1,0:T(8,128)S(1)}, u32[]{:S(2)}, u32[]{:S(2)}) %collective-permute-start.78) | collective-permute-done | bytes 32800 | tf_op jit(solution)/shard_map/ppermute | solution.py:31
  1301.3 25.9 %collective-permute-done.68 = f32[128,1024]{1,0:T(8,128)S(1)} collective-permute-done((f32[128,1024]{1,0:T(8,128)S(1)}, f32[128,1024]{1,0:T(8,128)S(1)}, u32[]{:S(2)}, u32[]{:S(2)}) %collective-permute-start.68) | collective-permute-done | bytes 524320 | tf_op jit(solution)/shard_map/ppermute | solution.py:31
  1351.3 19.4 %collective-permute-done.72 = f32[64,2048]{1,0:T(8,128)S(1)} collective-permute-done((f32[64,2048]{1,0:T(8,128)S(1)}, f32[64,2048]{1,0:T(8,128)S(1)}, u32[]{:S(2)}, u32[]{:S(2)}) %collective-permute-start.72) | collective-permute-done | bytes 524320 | tf_op jit(solution)/shard_map/ppermute | solution.py:31
  1370.7 24.8 %collective-permute-done.71 = f32[2,64,2048]{2,1,0:T(8,128)S(1)} collective-permute-done((f32[2,64,2048]{2,1,0:T(8,128)S(1)}, f32[2,64,2048]{2,1,0:T(8,128)S(1)}, u32[]{:S(2)}, u32[]{:S(2)}) %collective-permute-start.71) | collective-permute-done | bytes 1048608 | tf_op jit(solution)/shard_map/ppermute | solution.py:31
  (706 shorter events, 760.0 us)
Async XLA Ops:
  7.2 435.7 %all-gather.4.cloned.1.call-start = ((), (), s32[]{:S(2)}) async-start(), calls=%async_computation | async-start | bytes 8912896 | tf_op jit(solution)/shard_map/all_gather | solution.py:733
  18.1 579.6 %all-gather.6.cloned.1.call-start = ((), (), s32[]{:S(2)}) async-start(), calls=%async_computation.1 | async-start | bytes 8912896 | tf_op jit(solution)/shard_map/all_gather | solution.py:733
  37.3 79.3 %collective-permute-start.2 = (f32[128,2176]{1,0:T(8,128)}, f32[128,2176]{1,0:T(8,128)S(1)}, u32[]{:S(2)}, u32[]{:S(2)}) collective-permute-start(f32[128,2176]{1,0:T(8,128)} %bitcast.363), channel_id=1, source_target_pairs={{0,8},{1,9},{2,10},{3,11},{4,12},{5,13},{6,14},{7,15},{8,0},{9,1},... | collective-permute-start | bytes 3342344 | tf_op jit(solution)/shard_map/ppermute | solution.py:31
  39.4 85.6 %collective-permute-start.5 = (f32[128,1024]{1,0:T(8,128)S(1)}, f32[128,1024]{1,0:T(8,128)}, u32[]{:S(2)}, u32[]{:S(2)}) collective-permute-start(f32[128,1024]{1,0:T(8,128)S(1)} %dynamic-slice_bitcast_fusion.20), channel_id=1, source_target_pairs={{0,16},{16,0},{1,17},{17,1},{2,18},{18,2},{3,19},{19,3},{4,20},{20... | collective-permute-start | bytes 1572872 | tf_op jit(solution)/shard_map/ppermute | solution.py:27
  121.8 104.2 %collective-permute-start.3 = (f32[4,64,2176]{2,1,0:T(8,128)}, f32[4,64,2176]{2,1,0:T(8,128)}, u32[]{:S(2)}, u32[]{:S(2)}) collective-permute-start(f32[4,64,2176]{2,1,0:T(8,128)} %bitcast.422), channel_id=1, source_target_pairs={{0,1},{1,0},{2,3},{3,2},{4,5},{5,4},{6,7},{7,6},{8,9},{9,8},{10,11... | collective-permute-start | bytes 6684680 | tf_op jit(solution)/shard_map/ppermute | solution.py:31
  123.2 102.9 %collective-permute-start.4 = (f32[4,64,2176]{2,1,0:T(8,128)}, f32[4,64,2176]{2,1,0:T(8,128)}, u32[]{:S(2)}, u32[]{:S(2)}) collective-permute-start(f32[4,64,2176]{2,1,0:T(8,128)} %bitcast.423), channel_id=1, source_target_pairs={{0,2},{1,3},{2,0},{3,1},{4,6},{5,7},{6,4},{7,5},{8,10},{9,11},{10,... | collective-permute-start | bytes 6684680 | tf_op jit(solution)/shard_map/ppermute | solution.py:31
  124.4 481.9 %all-gather.8.cloned.1.call-start = ((), (), s32[]{:S(2)}) async-start(), calls=%async_computation.2 | async-start | bytes 8912896 | tf_op jit(solution)/shard_map/all_gather | solution.py:733
  229.8 116.3 %collective-permute-start.8 = (f32[4,64,2176]{2,1,0:T(8,128)}, f32[4,64,2176]{2,1,0:T(8,128)}, u32[]{:S(2)}, u32[]{:S(2)}) collective-permute-start(f32[4,64,2176]{2,1,0:T(8,128)} %broadcast_select_fusion), channel_id=1, source_target_pairs={{0,2},{1,3},{2,0},{3,1},{4,6},{5,7},{6,4},{7,5},{8,10},{9,11},{10,... | collective-permute-start | bytes 6684680 | tf_op jit(solution)/shard_map/ppermute | solution.py:38
  235.3 110.8 %collective-permute-start.9 = (f32[4,128,1024]{2,1,0:T(8,128)}, f32[4,128,1024]{2,1,0:T(8,128)}, u32[]{:S(2)}, u32[]{:S(2)}) collective-permute-start(f32[4,128,1024]{2,1,0:T(8,128)} %bitcast.436), channel_id=1, source_target_pairs={{0,1},{1,0},{2,3},{3,2},{4,5},{5,4},{6,7},{7,6},{8,9},{9,8},{10,11... | collective-permute-start | bytes 6291464 | tf_op jit(solution)/shard_map/ppermute | solution.py:31
  360.2 67.2 %collective-permute-start.14 = (f32[1024,2176]{1,0:T(8,128)}, f32[1024,2176]{1,0:T(8,128)}, u32[]{:S(2)}, u32[]{:S(2)}) collective-permute-start(f32[1024,2176]{1,0:T(8,128)} %bitcast.382), channel_id=1, source_target_pairs={{0,16},{16,0},{1,17},{17,1},{2,18},{18,2},{3,19},{19,3},{4,20},{20... | collective-permute-start | bytes 26738696 | tf_op jit(solution)/shard_map/ppermute | solution.py:27
  442.3 84.3 %collective-permute-start.22 = (f32[2048,1024]{1,0:T(8,128)}, f32[2048,1024]{1,0:T(8,128)}, u32[]{:S(2)}, u32[]{:S(2)}) collective-permute-start(f32[2048,1024]{1,0:T(8,128)} %bitcast.393), channel_id=1, source_target_pairs={{0,16},{16,0},{1,17},{17,1},{2,18},{18,2},{3,19},{19,3},{4,20},{20... | collective-permute-start | bytes 25165832 | tf_op jit(solution)/shard_map/ppermute | solution.py:27
  443.0 100.4 %collective-permute-start.20 = (f32[1024,2048]{1,0:T(8,128)}, f32[1024,2048]{1,0:T(8,128)}, u32[]{:S(2)}, u32[]{:S(2)}) collective-permute-start(f32[1024,2048]{1,0:T(8,128)} %all-gather.4.cloned.1.call-done.own), channel_id=1, source_target_pairs={{0,16},{16,0},{1,17},{17,1},{2,18},{18,2},{3,19},{19,3},{4,20},{20... | collective-permute-start | bytes 25165832 | tf_op jit(solution)/shard_map/ppermute | solution.py:27
  445.7 80.9 %collective-permute-start.23 = (f32[4,64,2048]{2,1,0:T(8,128)}, f32[4,64,2048]{2,1,0:T(8,128)}, u32[]{:S(2)}, u32[]{:S(2)}) collective-permute-start(f32[4,64,2048]{2,1,0:T(8,128)} %bitcast.438), channel_id=1, source_target_pairs={{0,1},{1,0},{2,3},{3,2},{4,5},{5,4},{6,7},{7,6},{8,9},{9,8},{10,11... | collective-permute-start | bytes 6291464 | tf_op jit(solution)/shard_map/ppermute | solution.py:31
  445.7 80.9 %collective-permute-start.24 = (f32[4,64,2048]{2,1,0:T(8,128)}, f32[4,64,2048]{2,1,0:T(8,128)}, u32[]{:S(2)}, u32[]{:S(2)}) collective-permute-start(f32[4,64,2048]{2,1,0:T(8,128)} %bitcast.439), channel_id=1, source_target_pairs={{0,2},{1,3},{2,0},{3,1},{4,6},{5,7},{6,4},{7,5},{8,10},{9,11},{10,... | collective-permute-start | bytes 6291464 | tf_op jit(solution)/shard_map/ppermute | solution.py:31
  450.5 76.2 %collective-permute-start.21 = (f32[4,64,1024]{2,1,0:T(8,128)S(1)}, f32[4,64,1024]{2,1,0:T(8,128)S(1)}, u32[]{:S(2)}, u32[]{:S(2)}) collective-permute-start(f32[4,64,1024]{2,1,0:T(8,128)S(1)} %broadcast_select_fusion.3), channel_id=1, source_target_pairs={{0,2},{1,3},{2,0},{3,1},{4,6},{5,7},{6,4},{7,5},{8,10},{9,11},{10,... | collective-permute-start | bytes 3145736 | tf_op jit(solution)/shard_map/ppermute | solution.py:38
  606.3 69.9 %collective-permute-start.29 = (f32[2048,1024]{1,0:T(8,128)}, f32[2048,1024]{1,0:T(8,128)}, u32[]{:S(2)}, u32[]{:S(2)}) collective-permute-start(f32[2048,1024]{1,0:T(8,128)} %all-gather.8.cloned.1.call-done.own), channel_id=1, source_target_pairs={{0,16},{16,0},{1,17},{17,1},{2,18},{18,2},{3,19},{19,3},{4,20},{20... | collective-permute-start | bytes 25165832 | tf_op jit(solution)/shard_map/ppermute | solution.py:27
  870.7 123.1 %collective-permute-start.43 = (f32[2048,1024]{1,0:T(8,128)}, f32[2048,1024]{1,0:T(8,128)}, u32[]{:S(2)}, u32[]{:S(2)}) collective-permute-start(f32[2048,1024]{1,0:T(8,128)} %shard_map.423), channel_id=1, source_target_pairs={{0,16},{16,0},{1,17},{17,1},{2,18},{18,2},{3,19},{19,3},{4,20},{20... | collective-permute-start | bytes 25165832 | tf_op jit(solution)/shard_map/ppermute | solution.py:27
  945.0 108.5 %collective-permute-start.49 = (f32[1024,2048]{1,0:T(8,128)}, f32[1024,2048]{1,0:T(8,128)}, u32[]{:S(2)}, u32[]{:S(2)}) collective-permute-start(f32[1024,2048]{1,0:T(8,128)} %shard_map.426), channel_id=1, source_target_pairs={{0,16},{16,0},{1,17},{17,1},{2,18},{18,2},{3,19},{19,3},{4,20},{20... | collective-permute-start | bytes 25165832 | tf_op jit(solution)/shard_map/ppermute | solution.py:27
  1190.2 91.1 %collective-permute-start.65 = (f32[4,64,2048]{2,1,0:T(8,128)}, f32[4,64,2048]{2,1,0:T(8,128)}, u32[]{:S(2)}, u32[]{:S(2)}) collective-permute-start(f32[4,64,2048]{2,1,0:T(8,128)} %get-tuple-element.291), channel_id=1, source_target_pairs={{0,1},{1,0},{2,3},{3,2},{4,5},{5,4},{6,7},{7,6},{8,9},{9,8},{10,11... | collective-permute-start | bytes 6291464 | tf_op jit(solution)/shard_map/ppermute | solution.py:31
  1191.0 90.3 %collective-permute-start.66 = (f32[4,64,2048]{2,1,0:T(8,128)}, f32[4,64,2048]{2,1,0:T(8,128)}, u32[]{:S(2)}, u32[]{:S(2)}) collective-permute-start(f32[4,64,2048]{2,1,0:T(8,128)} %get-tuple-element.292), channel_id=1, source_target_pairs={{0,2},{1,3},{2,0},{3,1},{4,6},{5,7},{6,4},{7,5},{8,10},{9,11},{10,... | collective-permute-start | bytes 6291464 | tf_op jit(solution)/shard_map/ppermute | solution.py:31
  1195.6 85.7 %collective-permute-start.62 = (f32[4,64,2048]{2,1,0:T(8,128)}, f32[4,64,2048]{2,1,0:T(8,128)}, u32[]{:S(2)}, u32[]{:S(2)}) collective-permute-start(f32[4,64,2048]{2,1,0:T(8,128)} %dynamic-slice_bitcast_fusion), channel_id=1, source_target_pairs={{0,1},{1,0},{2,3},{3,2},{4,5},{5,4},{6,7},{7,6},{8,9},{9,8},{10,11... | collective-permute-start | bytes 6291464 | tf_op jit(solution)/shard_map/ppermute | solution.py:38
  1203.4 77.9 %collective-permute-start.63 = (f32[2,128,1024]{2,1,0:T(8,128)}, f32[2,128,1024]{2,1,0:T(8,128)}, u32[]{:S(2)}, u32[]{:S(2)}) collective-permute-start(f32[2,128,1024]{2,1,0:T(8,128)} %dynamic-slice_bitcast_fusion.8), channel_id=1, source_target_pairs={{0,8},{1,9},{2,10},{3,11},{4,12},{5,13},{6,14},{7,15},{8,0},{9,1},... | collective-permute-start | bytes 3145736 | tf_op jit(solution)/shard_map/ppermute | solution.py:31
  1273.8 168.8 %collective-permute-start.33 = (f32[256,1024]{1,0:T(8,128)}, f32[256,1024]{1,0:T(8,128)}, u32[]{:S(2)}, u32[]{:S(2)}) collective-permute-start(f32[256,1024]{1,0:T(8,128)} %get-tuple-element.409), channel_id=1, source_target_pairs={{0,16},{16,0},{1,17},{17,1},{2,18},{18,2},{3,19},{19,3},{4,20},{20... | collective-permute-start | bytes 3145736 | tf_op jit(solution)/shard_map/ppermute | solution.py:27
  1327.1 120.5 %collective-permute-start.58 = (f32[256,1024]{1,0:T(8,128)}, f32[256,1024]{1,0:T(8,128)}, u32[]{:S(2)}, u32[]{:S(2)}) collective-permute-start(f32[256,1024]{1,0:T(8,128)} %get-tuple-element.401), channel_id=1, source_target_pairs={{0,16},{16,0},{1,17},{17,1},{2,18},{18,2},{3,19},{19,3},{4,20},{20... | collective-permute-start | bytes 3145736 | tf_op jit(solution)/shard_map/ppermute | solution.py:27
  (213 other events, 4596.1 us)
Sparse Core Ops, SparseCore 0:
  18.2 195.4 all-gather.3
  217.1 148.0 all-gather.5
  443.0 132.3 all-gather.7
